TPU v7x, 512 devices: a whole 4x8x8 slice. The times are simulated.
512 devices in a mesh: brick: 32 (over z, x), group: 16 (over y, core).
Axes of the slice: x: 4, y: 8, z: 8, core: 2. Of those that a mesh axis runs over, the one named last changes fastest.
Arguments:
- right_side: float32 [512, 256, 128], P('brick', 'group'), may hold values from -8 to 8
- mass_coef: float32 [512, 256, 128], P('brick', 'group'), may hold values from 0.25 to 4
- face_coef: float32 [512, 256, 128], P('brick', 'group'), may hold values from 0.25 to 4
Outputs:
- fine_fix: float32 [512, 256, 128], P('brick', 'group')
- middle_fix: float32 [256, 128, 64], P('brick', 'group')
- coarse_fix: float32 [128, 64, 32], P('brick', 'group')
- coarse_rhs: float32 [64, 32, 16], P('brick')
All inputs are finite; a program needn't handle non-finite values.
Results may differ from a plain program's by a relative error of at most 0.00019.
Values sent between devices are 32-bit elements; how exact they have to be, the bound alone decides.
A program may use at most 64 MiB of HBM per device.

v0:
```python
import jax
import jax.numpy as jnp
from jax import lax
from jax.sharding import PartitionSpec as P

LEVELS = 3


stencil_weight = 0.25
center_value = 1.1
half_width = 0.8
ratio_sigma = center_value / half_width
first_rho = 1.0 / ratio_sigma
second_rho = 1.0 / (2.0 * ratio_sigma - first_rho)
carry_factor = second_rho * first_rho
push_factor = 2.0 * second_rho / half_width


def with_halo(cells, sides, width):
    for axis, dim in sides:
        count = lax.axis_size(axis)
        ends = count - 1
        head = lax.slice_in_dim(cells, 0, width, axis=dim)
        tail = lax.slice_in_dim(cells, cells.shape[dim] - width, cells.shape[dim], axis=dim)
        cells = jnp.concatenate(
            [
                lax.ppermute(tail, axis, [(i, (i + 1) % count) for i in range(ends)]),
                cells,
                lax.ppermute(head, axis, [((i + 1) % count, i) for i in range(ends)]),
            ],
            axis=dim,
        )
    return cells


def interior(field):
    return field[1:-1, 1:-1, :]


def neighbours(field):
    padded = jnp.pad(field, ((0, 0), (0, 0), (1, 1)))
    return [
        field[2:, 1:-1, :],
        field[:-2, 1:-1, :],
        field[1:-1, 2:, :],
        field[1:-1, :-2, :],
        padded[1:-1, 1:-1, 2:],
        padded[1:-1, 1:-1, :-2],
    ]


def face_weights(face_coef):
    center = interior(face_coef)
    return [stencil_weight * 0.5 * (center + beside) for beside in neighbours(face_coef)]


def operate(field, mass_inner, weights_list):
    center = interior(field)
    total = mass_inner * center
    for weight_term, beside in zip(weights_list, neighbours(field)):
        total = total + weight_term * (center - beside)
    return total


def diagonal_of(mass_inner, weights_list):
    total = mass_inner
    for weight_term in weights_list:
        total = total + weight_term
    return total


def restrict(field):
    shaped = field.reshape(field.shape[0] // 2, 2, field.shape[1] // 2, 2, field.shape[2] // 2, 2)
    return shaped.mean(axis=(1, 3, 5))


def level_each(source, mass_coef, face_coef):
    face_loop = with_halo(face_coef, (("brick", 0), ("group", 1)), 1)
    weights_list = face_weights(face_loop)
    diagonal = diagonal_of(mass_coef, weights_list)
    first_step = source / diagonal / center_value
    first_loop = with_halo(first_step, (("brick", 0), ("group", 1)), 1)
    first_resid = source - operate(first_loop, mass_coef, weights_list)
    second_iter = first_step + carry_factor * first_step + push_factor * first_resid / diagonal
    second_loop = with_halo(second_iter, (("brick", 0), ("group", 1)), 1)
    residual = source - operate(second_loop, mass_coef, weights_list)
    return (second_iter, residual)


def body(right_side, mass_coef, face_coef):
    source = right_side
    corrections = []
    for tier_index in range(LEVELS):
        correction, residual = level_each(source, mass_coef, face_coef)
        corrections.append(correction)
        source = restrict(residual)
        mass_coef = restrict(mass_coef)
        face_coef = restrict(face_coef)
    coarse_rhs = lax.all_gather(source, "group", axis=1, tiled=True)
    return (corrections[0], corrections[1], corrections[2], coarse_rhs)


def solution(mesh):
    placed = (P("brick", "group", None), P("brick", "group", None), P("brick", "group", None))
    return jax.shard_map(
        body,
        mesh=mesh,
        in_specs=placed,
        out_specs=(
            P("brick", "group", None),
            P("brick", "group", None),
            P("brick", "group", None),
            P("brick", None, None),
        ),
        check_vma=False,
    )
```

profile of v0, /device:TPU:223, one launch (start us, length us, event | category | flops | bytes accessed | tf_op | source)
XLA Modules:
  0.0 227.1 jit_solution(2784615398781662891)
XLA Ops:
  0.6 0.7 fusion.151
  1.4 5.1 %collective-permute-start.1 = (f32[1,16,128]{2,1,0:T(8,128)S(1)}, f32[1,16,128]{2,1,0:T(8,128)S(1)}, u32[]{:S(2)}, u32[]{:S(2)}) collective-permute-start(f32[1,16,128]{2,1,0:T(8,128)S(1)} %get-tuple-element.20), channel_id=1, source_target_pairs={{0,16},{16,32},{32,48},{48,64},{64,80},{80,96},{96,112},{112,128},... | collective-permute-start | bytes 24584 | tf_op jit(solution)/shard_map/ppermute | solution.py:27
  6.5 1.9 collective-permute-start
  8.4 0.9 constant_dynamic-update-slice_fusion.1
  9.3 4.8 %collective-permute-done = f32[1,16,128]{2,1,0:T(8,128)S(1)} collective-permute-done((f32[1,16,128]{2,1,0:T(8,128)S(1)}, f32[1,16,128]{2,1,0:T(8,128)S(1)}, u32[]{:S(2)}, u32[]{:S(2)}) %collective-permute-start) | collective-permute-done | bytes 8224 | tf_op jit(solution)/shard_map/ppermute | solution.py:29
  14.2 6.4 %collective-permute-start.3 = (f32[18,1,128]{2,1,0:T(1,128)S(1)}, f32[18,1,128]{2,1,0:T(1,128)S(1)}, u32[]{:S(2)}, u32[]{:S(2)}) collective-permute-start(f32[18,1,128]{2,1,0:T(1,128)S(1)} %get-tuple-element.14), channel_id=1, source_target_pairs={{0,1},{1,2},{2,3},{3,4},{4,5},{5,6},{6,7},{7,8},{8,9},{9,10},{10,1... | collective-permute-start | bytes 27656 | tf_op jit(solution)/shard_map/ppermute | solution.py:27
  20.7 2.1 collective-permute-start.2
  22.7 10.6 %reshape.33 = f32[8,2,8,2,64,2]{5,4,3,2,1,0:T(8,128)} reshape(f32[16,16,128]{2,1,0:T(8,128)} %param.5) | data formatting | bytes 262144 | tf_op jit(solution)/shard_map/reshape | solution.py:73
  33.3 4.0 %reduce_sum.65 = f32[8,8,64]{2,1,0:T(8,128)S(1)} reduce(f32[8,2,8,2,64,2]{5,4,3,2,1,0:T(8,128)} %reshape.33, f32[]{:T(128)} %constant.15.clone.1), dimensions={1,3,5}, to_apply=%region_2.3 | reduce | flops 28672 | bytes 147460 | tf_op jit(solution)/shard_map/reduce_sum | solution.py:74
  37.3 0.3 select_maximum_fusion.8
  37.8 1.9 collective-permute-start.5
  39.7 3.4 %collective-permute-start.4 = (f32[1,16,128]{2,1,0:T(8,128)S(1)}, f32[1,16,128]{2,1,0:T(8,128)S(1)}, u32[]{:S(2)}, u32[]{:S(2)}) collective-permute-start(f32[1,16,128]{2,1,0:T(8,128)S(1)} %get-tuple-element.19), channel_id=1, source_target_pairs={{16,0},{32,16},{48,32},{64,48},{80,64},{96,80},{112,96},{128,112},... | collective-permute-start | bytes 24584 | tf_op jit(solution)/shard_map/ppermute | solution.py:29
  43.1 4.4 %collective-permute-done.4 = f32[1,16,128]{2,1,0:T(8,128)S(1)} collective-permute-done((f32[1,16,128]{2,1,0:T(8,128)S(1)}, f32[1,16,128]{2,1,0:T(8,128)S(1)}, u32[]{:S(2)}, u32[]{:S(2)}) %collective-permute-start.4) | collective-permute-done | bytes 8224 | tf_op jit(solution)/shard_map/ppermute | solution.py:29
  47.5 5.9 %collective-permute-start.7 = (f32[18,1,128]{2,1,0:T(1,128)S(1)}, f32[18,1,128]{2,1,0:T(1,128)S(1)}, u32[]{:S(2)}, u32[]{:S(2)}) collective-permute-start(f32[18,1,128]{2,1,0:T(1,128)S(1)} %get-tuple-element.12), channel_id=1, source_target_pairs={{0,1},{1,2},{2,3},{3,4},{4,5},{5,6},{6,7},{7,8},{8,9},{9,10},{10,1... | collective-permute-start | bytes 27656 | tf_op jit(solution)/shard_map/ppermute | solution.py:27
  53.4 1.9 collective-permute-start.6
  55.4 1.9 collective-permute-start.13
  57.3 3.4 %collective-permute-start.12 = (f32[1,8,64]{2,1,0:T(8,128)S(1)}, f32[1,8,64]{2,1,0:T(8,128)S(1)}, u32[]{:S(2)}, u32[]{:S(2)}) collective-permute-start(f32[1,8,64]{2,1,0:T(8,128)S(1)} %get-tuple-element.35), channel_id=1, source_target_pairs={{16,0},{32,16},{48,32},{64,48},{80,64},{96,80},{112,96},{128,112},... | collective-permute-start | bytes 6152 | tf_op jit(solution)/shard_map/ppermute | solution.py:29
  60.7 9.8 %reshape.32 = f32[8,2,8,2,64,2]{5,4,3,2,1,0:T(8,128)} reshape(f32[16,16,128]{2,1,0:T(8,128)S(1)} %copy-done.2) | data formatting | bytes 262144 | tf_op jit(solution)/shard_map/reshape | solution.py:73
  70.5 1.1 div.78
  71.6 4.0 %reduce_sum.64 = f32[8,8,64]{2,1,0:T(8,128)S(1)} reduce(f32[8,2,8,2,64,2]{5,4,3,2,1,0:T(8,128)} %reshape.32, f32[]{:T(128)} %constant.15.clone.1), dimensions={1,3,5}, to_apply=%region_1.2 | reduce | flops 28672 | bytes 147460 | tf_op jit(solution)/shard_map/reduce_sum | solution.py:74
  75.8 0.3 select_maximum_fusion.4
  76.0 0.4 fusion.23
  76.4 5.2 %collective-permute-start.9 = (f32[1,16,128]{2,1,0:T(8,128)S(1)}, f32[1,16,128]{2,1,0:T(8,128)S(1)}, u32[]{:S(2)}, u32[]{:S(2)}) collective-permute-start(f32[1,16,128]{2,1,0:T(8,128)S(1)} %get-tuple-element.16), channel_id=1, source_target_pairs={{0,16},{16,32},{32,48},{48,64},{64,80},{80,96},{96,112},{112,128},... | collective-permute-start | bytes 24584 | tf_op jit(solution)/shard_map/ppermute | solution.py:27
  81.7 1.9 collective-permute-start.8
  83.6 5.4 %collective-permute-start.15 = (f32[10,1,64]{2,1,0:T(1,128)S(1)}, f32[10,1,64]{2,1,0:T(1,128)S(1)}, u32[]{:S(2)}, u32[]{:S(2)}) collective-permute-start(f32[10,1,64]{2,1,0:T(1,128)S(1)} %get-tuple-element.26), channel_id=1, source_target_pairs={{0,1},{1,2},{2,3},{3,4},{4,5},{5,6},{6,7},{7,8},{8,9},{9,10},{10,1... | collective-permute-start | bytes 7688 | tf_op jit(solution)/shard_map/ppermute | solution.py:27
  89.1 1.9 collective-permute-start.14
  91.0 4.9 %collective-permute-start.11 = (f32[18,1,128]{2,1,0:T(1,128)S(1)}, f32[18,1,128]{2,1,0:T(1,128)S(1)}, u32[]{:S(2)}, u32[]{:S(2)}) collective-permute-start(f32[18,1,128]{2,1,0:T(1,128)S(1)} %get-tuple-element.10), channel_id=1, source_target_pairs={{0,1},{1,2},{2,3},{3,4},{4,5},{5,6},{6,7},{7,8},{8,9},{9,10},{10,1... | collective-permute-start | bytes 27656 | tf_op jit(solution)/shard_map/ppermute | solution.py:27
  96.0 1.9 collective-permute-start.10
  98.1 4.1 %collective-permute-done.10 = f32[18,1,128]{2,1,0:T(1,128)S(1)} collective-permute-done((f32[18,1,128]{2,1,0:T(1,128)S(1)}, f32[18,1,128]{2,1,0:T(1,128)S(1)}, u32[]{:S(2)}, u32[]{:S(2)}) %collective-permute-start.10) | collective-permute-done | bytes 9248 | tf_op jit(solution)/shard_map/ppermute | solution.py:29
  102.2 0.3 select_maximum_fusion
  102.4 0.3 fusion.3
  102.7 9.8 %reshape.31 = f32[8,2,8,2,64,2]{5,4,3,2,1,0:T(8,128)} reshape(f32[16,16,128]{2,1,0:T(8,128)S(1)} %fusion.3) | data formatting | bytes 262144 | tf_op jit(solution)/shard_map/reshape | solution.py:73
  112.5 4.0 %reduce_sum.63 = f32[8,8,64]{2,1,0:T(8,128)S(1)} reduce(f32[8,2,8,2,64,2]{5,4,3,2,1,0:T(8,128)} %reshape.31, f32[]{:T(128)} %constant.15.clone.1), dimensions={1,3,5}, to_apply=%region_0.1 | reduce | flops 28672 | bytes 147460 | tf_op jit(solution)/shard_map/reduce_sum | solution.py:74
  116.7 6.9 %collective-permute-start.17 = (f32[1,8,64]{2,1,0:T(8,128)S(1)}, f32[1,8,64]{2,1,0:T(8,128)S(1)}, u32[]{:S(2)}, u32[]{:S(2)}) collective-permute-start(f32[1,8,64]{2,1,0:T(8,128)S(1)} %get-tuple-element.32), channel_id=1, source_target_pairs={{0,16},{16,32},{32,48},{48,64},{64,80},{80,96},{96,112},{112,128},... | collective-permute-start | bytes 6152 | tf_op jit(solution)/shard_map/ppermute | solution.py:27
  123.5 1.9 collective-permute-start.16
  125.5 5.7 %collective-permute-done.16 = f32[1,8,64]{2,1,0:T(8,128)S(1)} collective-permute-done((f32[1,8,64]{2,1,0:T(8,128)S(1)}, f32[1,8,64]{2,1,0:T(8,128)S(1)}, u32[]{:S(2)}, u32[]{:S(2)}) %collective-permute-start.16) | collective-permute-done | bytes 2080 | tf_op jit(solution)/shard_map/ppermute | solution.py:29
  131.2 3.4 %collective-permute-start.19 = (f32[10,1,64]{2,1,0:T(1,128)S(1)}, f32[10,1,64]{2,1,0:T(1,128)S(1)}, u32[]{:S(2)}, u32[]{:S(2)}) collective-permute-start(f32[10,1,64]{2,1,0:T(1,128)S(1)} %get-tuple-element.24), channel_id=1, source_target_pairs={{0,1},{1,2},{2,3},{3,4},{4,5},{5,6},{6,7},{7,8},{8,9},{9,10},{10,1... | collective-permute-start | bytes 7688 | tf_op jit(solution)/shard_map/ppermute | solution.py:27
  134.6 1.9 collective-permute-start.18
  136.6 1.9 collective-permute-start.25
  138.5 3.4 %collective-permute-start.24 = (f32[1,4,32]{2,1,0:T(4,128)S(1)}, f32[1,4,32]{2,1,0:T(4,128)S(1)}, u32[]{:S(2)}, u32[]{:S(2)}) collective-permute-start(f32[1,4,32]{2,1,0:T(4,128)S(1)} %get-tuple-element.47), channel_id=1, source_target_pairs={{16,0},{32,16},{48,32},{64,48},{80,64},{96,80},{112,96},{128,112},... | collective-permute-start | bytes 1544 | tf_op jit(solution)/shard_map/ppermute | solution.py:29
  142.1 5.2 %collective-permute-start.21 = (f32[1,8,64]{2,1,0:T(8,128)S(1)}, f32[1,8,64]{2,1,0:T(8,128)S(1)}, u32[]{:S(2)}, u32[]{:S(2)}) collective-permute-start(f32[1,8,64]{2,1,0:T(8,128)S(1)} %get-tuple-element.28), channel_id=1, source_target_pairs={{0,16},{16,32},{32,48},{48,64},{64,80},{80,96},{96,112},{112,128},... | collective-permute-start | bytes 6152 | tf_op jit(solution)/shard_map/ppermute | solution.py:27
  147.4 1.9 collective-permute-start.20
  149.3 5.4 %collective-permute-start.27 = (f32[6,1,32]{2,1,0:T(1,128)S(1)}, f32[6,1,32]{2,1,0:T(1,128)S(1)}, u32[]{:S(2)}, u32[]{:S(2)}) collective-permute-start(f32[6,1,32]{2,1,0:T(1,128)S(1)} %get-tuple-element.40), channel_id=1, source_target_pairs={{0,1},{1,2},{2,3},{3,4},{4,5},{5,6},{6,7},{7,8},{8,9},{9,10},{10,1... | collective-permute-start | bytes 2312 | tf_op jit(solution)/shard_map/ppermute | solution.py:27
  154.8 1.9 collective-permute-start.26
  156.7 4.9 %collective-permute-start.23 = (f32[10,1,64]{2,1,0:T(1,128)S(1)}, f32[10,1,64]{2,1,0:T(1,128)S(1)}, u32[]{:S(2)}, u32[]{:S(2)}) collective-permute-start(f32[10,1,64]{2,1,0:T(1,128)S(1)} %get-tuple-element.22), channel_id=1, source_target_pairs={{0,1},{1,2},{2,3},{3,4},{4,5},{5,6},{6,7},{7,8},{8,9},{9,10},{10,1... | collective-permute-start | bytes 7688 | tf_op jit(solution)/shard_map/ppermute | solution.py:27
  161.6 2.1 collective-permute-start.22
  163.9 1.1 div.76
  164.9 0.2 reduce_sum.67
  165.1 2.7 %collective-permute-done.22 = f32[10,1,64]{2,1,0:T(1,128)S(1)} collective-permute-done((f32[10,1,64]{2,1,0:T(1,128)S(1)}, f32[10,1,64]{2,1,0:T(1,128)S(1)}, u32[]{:S(2)}, u32[]{:S(2)}) %collective-permute-start.22) | collective-permute-done | bytes 2592 | tf_op jit(solution)/shard_map/ppermute | solution.py:29
  168.0 1.1 reshape.34
  169.3 6.9 %collective-permute-start.29 = (f32[1,4,32]{2,1,0:T(4,128)S(1)}, f32[1,4,32]{2,1,0:T(4,128)S(1)}, u32[]{:S(2)}, u32[]{:S(2)}) collective-permute-start(f32[1,4,32]{2,1,0:T(4,128)S(1)} %get-tuple-element.44), channel_id=1, source_target_pairs={{0,16},{16,32},{32,48},{48,64},{64,80},{80,96},{96,112},{112,128},... | collective-permute-start | bytes 1544 | tf_op jit(solution)/shard_map/ppermute | solution.py:27
  176.3 1.9 collective-permute-start.28
  178.2 5.7 %collective-permute-done.28 = f32[1,4,32]{2,1,0:T(4,128)S(1)} collective-permute-done((f32[1,4,32]{2,1,0:T(4,128)S(1)}, f32[1,4,32]{2,1,0:T(4,128)S(1)}, u32[]{:S(2)}, u32[]{:S(2)}) %collective-permute-start.28) | collective-permute-done | bytes 544 | tf_op jit(solution)/shard_map/ppermute | solution.py:29
  183.9 3.6 %collective-permute-start.31 = (f32[6,1,32]{2,1,0:T(1,128)S(1)}, f32[6,1,32]{2,1,0:T(1,128)S(1)}, u32[]{:S(2)}, u32[]{:S(2)}) collective-permute-start(f32[6,1,32]{2,1,0:T(1,128)S(1)} %get-tuple-element.38), channel_id=1, source_target_pairs={{0,1},{1,2},{2,3},{3,4},{4,5},{5,6},{6,7},{7,8},{8,9},{9,10},{10,1... | collective-permute-start | bytes 2312 | tf_op jit(solution)/shard_map/ppermute | solution.py:27
  187.6 1.9 collective-permute-start.30
  189.5 4.2 %collective-permute-done.30 = f32[6,1,32]{2,1,0:T(1,128)S(1)} collective-permute-done((f32[6,1,32]{2,1,0:T(1,128)S(1)}, f32[6,1,32]{2,1,0:T(1,128)S(1)}, u32[]{:S(2)}, u32[]{:S(2)}) %collective-permute-start.30) | collective-permute-done | bytes 800 | tf_op jit(solution)/shard_map/ppermute | solution.py:29
  193.9 1.9 collective-permute-start.33
  195.8 3.4 %collective-permute-start.32 = (f32[1,4,32]{2,1,0:T(4,128)S(1)}, f32[1,4,32]{2,1,0:T(4,128)S(1)}, u32[]{:S(2)}, u32[]{:S(2)}) collective-permute-start(f32[1,4,32]{2,1,0:T(4,128)S(1)} %get-tuple-element.43), channel_id=1, source_target_pairs={{16,0},{32,16},{48,32},{64,48},{80,64},{96,80},{112,96},{128,112},... | collective-permute-start | bytes 1544 | tf_op jit(solution)/shard_map/ppermute | solution.py:29
  199.2 4.3 %collective-permute-done.32 = f32[1,4,32]{2,1,0:T(4,128)S(1)} collective-permute-done((f32[1,4,32]{2,1,0:T(4,128)S(1)}, f32[1,4,32]{2,1,0:T(4,128)S(1)}, u32[]{:S(2)}, u32[]{:S(2)}) %collective-permute-start.32) | collective-permute-done | bytes 544 | tf_op jit(solution)/shard_map/ppermute | solution.py:29
  203.5 3.1 %collective-permute-start.35 = (f32[6,1,32]{2,1,0:T(1,128)S(1)}, f32[6,1,32]{2,1,0:T(1,128)S(1)}, u32[]{:S(2)}, u32[]{:S(2)}) collective-permute-start(f32[6,1,32]{2,1,0:T(1,128)S(1)} %get-tuple-element.36), channel_id=1, source_target_pairs={{0,1},{1,2},{2,3},{3,4},{4,5},{5,6},{6,7},{7,8},{8,9},{9,10},{10,1... | collective-permute-start | bytes 2312 | tf_op jit(solution)/shard_map/ppermute | solution.py:27
  206.6 1.9 collective-permute-start.34
  208.5 4.2 %collective-permute-done.34 = f32[6,1,32]{2,1,0:T(1,128)S(1)} collective-permute-done((f32[6,1,32]{2,1,0:T(1,128)S(1)}, f32[6,1,32]{2,1,0:T(1,128)S(1)}, u32[]{:S(2)}, u32[]{:S(2)}) %collective-permute-start.34) | collective-permute-done | bytes 800 | tf_op jit(solution)/shard_map/ppermute | solution.py:29
  213.1 13.3 %all_gather.3 = f32[2,32,16]{2,0,1:T(2,128)S(1)} all-gather(f32[2,2,16]{2,0,1:T(2,128)S(1)} %copy.7), channel_id=1, replica_groups=mesh['brick'=32,'group'=16] {'group'}, dimensions={1}, use_global_device_ids=true | all-gather | bytes 4352 | tf_op jit(solution)/shard_map/all_gather | solution.py:99
  226.5 0.7 copy.8
  (79 shorter events, 2.1 us)
Async XLA Ops:
  1.4 7.1 %collective-permute-start.1 = (f32[1,16,128]{2,1,0:T(8,128)S(1)}, f32[1,16,128]{2,1,0:T(8,128)S(1)}, u32[]{:S(2)}, u32[]{:S(2)}) collective-permute-start(f32[1,16,128]{2,1,0:T(8,128)S(1)} %get-tuple-element.20), channel_id=1, source_target_pairs={{0,16},{16,32},{32,48},{48,64},{64,80},{80,96},{96,112},{112,128},... | collective-permute-start | bytes 24584 | tf_op jit(solution)/shard_map/ppermute | solution.py:27
  6.5 7.7 %collective-permute-start = (f32[1,16,128]{2,1,0:T(8,128)S(1)}, f32[1,16,128]{2,1,0:T(8,128)S(1)}, u32[]{:S(2)}, u32[]{:S(2)}) collective-permute-start(f32[1,16,128]{2,1,0:T(8,128)S(1)} %get-tuple-element.21), channel_id=1, source_target_pairs={{16,0},{32,16},{48,32},{64,48},{80,64},{96,80},{112,96},{128,112},... | collective-permute-start | bytes 24584 | tf_op jit(solution)/shard_map/ppermute | solution.py:29
  14.2 23.1 %collective-permute-start.3 = (f32[18,1,128]{2,1,0:T(1,128)S(1)}, f32[18,1,128]{2,1,0:T(1,128)S(1)}, u32[]{:S(2)}, u32[]{:S(2)}) collective-permute-start(f32[18,1,128]{2,1,0:T(1,128)S(1)} %get-tuple-element.14), channel_id=1, source_target_pairs={{0,1},{1,2},{2,3},{3,4},{4,5},{5,6},{6,7},{7,8},{8,9},{9,10},{10,1... | collective-permute-start | bytes 27656 | tf_op jit(solution)/shard_map/ppermute | solution.py:27
  20.6 17.0 %copy-start = (f32[16,16,128]{2,1,0:T(8,128)S(1)}, f32[16,16,128]{2,1,0:T(8,128)}, u32[]{:S(2)}) copy-start(f32[16,16,128]{2,1,0:T(8,128)} %param.5) | copy-start | bytes 393220
  20.6 17.0 %copy-start.2 = (f32[16,16,128]{2,1,0:T(8,128)S(1)}, f32[16,16,128]{2,1,0:T(8,128)}, u32[]{:S(2)}) copy-start(f32[16,16,128]{2,1,0:T(8,128)} %param.4) | copy-start | bytes 393220
  20.6 17.0 %copy-start.3 = (f32[16,16,128]{2,1,0:T(8,128)S(1)}, f32[16,16,128]{2,1,0:T(8,128)}, u32[]{:S(2)}) copy-start(f32[16,16,128]{2,1,0:T(8,128)} %param.3) | copy-start | bytes 393220
  20.7 16.6 %collective-permute-start.2 = (f32[18,1,128]{2,1,0:T(1,128)S(1)}, f32[18,1,128]{2,1,0:T(1,128)S(1)}, u32[]{:S(2)}, u32[]{:S(2)}) collective-permute-start(f32[18,1,128]{2,1,0:T(1,128)S(1)} %get-tuple-element.15), channel_id=1, source_target_pairs={{1,0},{2,1},{3,2},{4,3},{5,4},{6,5},{7,6},{8,7},{9,8},{10,9},{11,1... | collective-permute-start | bytes 27656 | tf_op jit(solution)/shard_map/ppermute | solution.py:29
  37.8 5.3 %collective-permute-start.5 = (f32[1,16,128]{2,1,0:T(8,128)S(1)}, f32[1,16,128]{2,1,0:T(8,128)S(1)}, u32[]{:S(2)}, u32[]{:S(2)}) collective-permute-start(f32[1,16,128]{2,1,0:T(8,128)S(1)} %get-tuple-element.18), channel_id=1, source_target_pairs={{0,16},{16,32},{32,48},{48,64},{64,80},{80,96},{96,112},{112,128},... | collective-permute-start | bytes 24584 | tf_op jit(solution)/shard_map/ppermute | solution.py:27
  39.7 7.8 %collective-permute-start.4 = (f32[1,16,128]{2,1,0:T(8,128)S(1)}, f32[1,16,128]{2,1,0:T(8,128)S(1)}, u32[]{:S(2)}, u32[]{:S(2)}) collective-permute-start(f32[1,16,128]{2,1,0:T(8,128)S(1)} %get-tuple-element.19), channel_id=1, source_target_pairs={{16,0},{32,16},{48,32},{64,48},{80,64},{96,80},{112,96},{128,112},... | collective-permute-start | bytes 24584 | tf_op jit(solution)/shard_map/ppermute | solution.py:29
  47.5 28.2 %collective-permute-start.7 = (f32[18,1,128]{2,1,0:T(1,128)S(1)}, f32[18,1,128]{2,1,0:T(1,128)S(1)}, u32[]{:S(2)}, u32[]{:S(2)}) collective-permute-start(f32[18,1,128]{2,1,0:T(1,128)S(1)} %get-tuple-element.12), channel_id=1, source_target_pairs={{0,1},{1,2},{2,3},{3,4},{4,5},{5,6},{6,7},{7,8},{8,9},{9,10},{10,1... | collective-permute-start | bytes 27656 | tf_op jit(solution)/shard_map/ppermute | solution.py:27
  53.4 22.3 %collective-permute-start.6 = (f32[18,1,128]{2,1,0:T(1,128)S(1)}, f32[18,1,128]{2,1,0:T(1,128)S(1)}, u32[]{:S(2)}, u32[]{:S(2)}) collective-permute-start(f32[18,1,128]{2,1,0:T(1,128)S(1)} %get-tuple-element.13), channel_id=1, source_target_pairs={{1,0},{2,1},{3,2},{4,3},{5,4},{6,5},{7,6},{8,7},{9,8},{10,9},{11,1... | collective-permute-start | bytes 27656 | tf_op jit(solution)/shard_map/ppermute | solution.py:29
  55.4 28.2 %collective-permute-start.13 = (f32[1,8,64]{2,1,0:T(8,128)S(1)}, f32[1,8,64]{2,1,0:T(8,128)S(1)}, u32[]{:S(2)}, u32[]{:S(2)}) collective-permute-start(f32[1,8,64]{2,1,0:T(8,128)S(1)} %get-tuple-element.34), channel_id=1, source_target_pairs={{0,16},{16,32},{32,48},{48,64},{64,80},{80,96},{96,112},{112,128},... | collective-permute-start | bytes 6152 | tf_op jit(solution)/shard_map/ppermute | solution.py:27
  57.3 26.3 %collective-permute-start.12 = (f32[1,8,64]{2,1,0:T(8,128)S(1)}, f32[1,8,64]{2,1,0:T(8,128)S(1)}, u32[]{:S(2)}, u32[]{:S(2)}) collective-permute-start(f32[1,8,64]{2,1,0:T(8,128)S(1)} %get-tuple-element.35), channel_id=1, source_target_pairs={{16,0},{32,16},{48,32},{64,48},{80,64},{96,80},{112,96},{128,112},... | collective-permute-start | bytes 6152 | tf_op jit(solution)/shard_map/ppermute | solution.py:29
  76.4 40.1 %copy-start.1 = (f32[16,16,128]{2,1,0:T(8,128)}, f32[16,16,128]{2,1,0:T(8,128)S(1)}, u32[]{:S(2)}) copy-start(f32[16,16,128]{2,1,0:T(8,128)S(1)} %fusion.23) | copy-start | bytes 393220
  76.4 14.6 %collective-permute-start.9 = (f32[1,16,128]{2,1,0:T(8,128)S(1)}, f32[1,16,128]{2,1,0:T(8,128)S(1)}, u32[]{:S(2)}, u32[]{:S(2)}) collective-permute-start(f32[1,16,128]{2,1,0:T(8,128)S(1)} %get-tuple-element.16), channel_id=1, source_target_pairs={{0,16},{16,32},{32,48},{48,64},{64,80},{80,96},{96,112},{112,128},... | collective-permute-start | bytes 24584 | tf_op jit(solution)/shard_map/ppermute | solution.py:27
  81.7 9.3 %collective-permute-start.8 = (f32[1,16,128]{2,1,0:T(8,128)S(1)}, f32[1,16,128]{2,1,0:T(8,128)S(1)}, u32[]{:S(2)}, u32[]{:S(2)}) collective-permute-start(f32[1,16,128]{2,1,0:T(8,128)S(1)} %get-tuple-element.17), channel_id=1, source_target_pairs={{16,0},{32,16},{48,32},{64,48},{80,64},{96,80},{112,96},{128,112},... | collective-permute-start | bytes 24584 | tf_op jit(solution)/shard_map/ppermute | solution.py:29
  83.6 14.3 %collective-permute-start.15 = (f32[10,1,64]{2,1,0:T(1,128)S(1)}, f32[10,1,64]{2,1,0:T(1,128)S(1)}, u32[]{:S(2)}, u32[]{:S(2)}) collective-permute-start(f32[10,1,64]{2,1,0:T(1,128)S(1)} %get-tuple-element.26), channel_id=1, source_target_pairs={{0,1},{1,2},{2,3},{3,4},{4,5},{5,6},{6,7},{7,8},{8,9},{9,10},{10,1... | collective-permute-start | bytes 7688 | tf_op jit(solution)/shard_map/ppermute | solution.py:27
  89.1 8.9 %collective-permute-start.14 = (f32[10,1,64]{2,1,0:T(1,128)S(1)}, f32[10,1,64]{2,1,0:T(1,128)S(1)}, u32[]{:S(2)}, u32[]{:S(2)}) collective-permute-start(f32[10,1,64]{2,1,0:T(1,128)S(1)} %get-tuple-element.27), channel_id=1, source_target_pairs={{1,0},{2,1},{3,2},{4,3},{5,4},{6,5},{7,6},{8,7},{9,8},{10,9},{11,1... | collective-permute-start | bytes 7688 | tf_op jit(solution)/shard_map/ppermute | solution.py:29
  91.0 7.0 %collective-permute-start.11 = (f32[18,1,128]{2,1,0:T(1,128)S(1)}, f32[18,1,128]{2,1,0:T(1,128)S(1)}, u32[]{:S(2)}, u32[]{:S(2)}) collective-permute-start(f32[18,1,128]{2,1,0:T(1,128)S(1)} %get-tuple-element.10), channel_id=1, source_target_pairs={{0,1},{1,2},{2,3},{3,4},{4,5},{5,6},{6,7},{7,8},{8,9},{9,10},{10,1... | collective-permute-start | bytes 27656 | tf_op jit(solution)/shard_map/ppermute | solution.py:27
  96.0 6.2 %collective-permute-start.10 = (f32[18,1,128]{2,1,0:T(1,128)S(1)}, f32[18,1,128]{2,1,0:T(1,128)S(1)}, u32[]{:S(2)}, u32[]{:S(2)}) collective-permute-start(f32[18,1,128]{2,1,0:T(1,128)S(1)} %get-tuple-element.11), channel_id=1, source_target_pairs={{1,0},{2,1},{3,2},{4,3},{5,4},{6,5},{7,6},{8,7},{9,8},{10,9},{11,1... | collective-permute-start | bytes 27656 | tf_op jit(solution)/shard_map/ppermute | solution.py:29
  116.7 8.8 %collective-permute-start.17 = (f32[1,8,64]{2,1,0:T(8,128)S(1)}, f32[1,8,64]{2,1,0:T(8,128)S(1)}, u32[]{:S(2)}, u32[]{:S(2)}) collective-permute-start(f32[1,8,64]{2,1,0:T(8,128)S(1)} %get-tuple-element.32), channel_id=1, source_target_pairs={{0,16},{16,32},{32,48},{48,64},{64,80},{80,96},{96,112},{112,128},... | collective-permute-start | bytes 6152 | tf_op jit(solution)/shard_map/ppermute | solution.py:27
  123.5 7.7 %collective-permute-start.16 = (f32[1,8,64]{2,1,0:T(8,128)S(1)}, f32[1,8,64]{2,1,0:T(8,128)S(1)}, u32[]{:S(2)}, u32[]{:S(2)}) collective-permute-start(f32[1,8,64]{2,1,0:T(8,128)S(1)} %get-tuple-element.33), channel_id=1, source_target_pairs={{16,0},{32,16},{48,32},{64,48},{80,64},{96,80},{112,96},{128,112},... | collective-permute-start | bytes 6152 | tf_op jit(solution)/shard_map/ppermute | solution.py:29
  131.2 10.6 %collective-permute-start.19 = (f32[10,1,64]{2,1,0:T(1,128)S(1)}, f32[10,1,64]{2,1,0:T(1,128)S(1)}, u32[]{:S(2)}, u32[]{:S(2)}) collective-permute-start(f32[10,1,64]{2,1,0:T(1,128)S(1)} %get-tuple-element.24), channel_id=1, source_target_pairs={{0,1},{1,2},{2,3},{3,4},{4,5},{5,6},{6,7},{7,8},{8,9},{9,10},{10,1... | collective-permute-start | bytes 7688 | tf_op jit(solution)/shard_map/ppermute | solution.py:27
  134.6 7.3 %collective-permute-start.18 = (f32[10,1,64]{2,1,0:T(1,128)S(1)}, f32[10,1,64]{2,1,0:T(1,128)S(1)}, u32[]{:S(2)}, u32[]{:S(2)}) collective-permute-start(f32[10,1,64]{2,1,0:T(1,128)S(1)} %get-tuple-element.25), channel_id=1, source_target_pairs={{1,0},{2,1},{3,2},{4,3},{5,4},{6,5},{7,6},{8,7},{9,8},{10,9},{11,1... | collective-permute-start | bytes 7688 | tf_op jit(solution)/shard_map/ppermute | solution.py:29
  136.6 12.8 %collective-permute-start.25 = (f32[1,4,32]{2,1,0:T(4,128)S(1)}, f32[1,4,32]{2,1,0:T(4,128)S(1)}, u32[]{:S(2)}, u32[]{:S(2)}) collective-permute-start(f32[1,4,32]{2,1,0:T(4,128)S(1)} %get-tuple-element.46), channel_id=1, source_target_pairs={{0,16},{16,32},{32,48},{48,64},{64,80},{80,96},{96,112},{112,128},... | collective-permute-start | bytes 1544 | tf_op jit(solution)/shard_map/ppermute | solution.py:27
  138.5 10.8 %collective-permute-start.24 = (f32[1,4,32]{2,1,0:T(4,128)S(1)}, f32[1,4,32]{2,1,0:T(4,128)S(1)}, u32[]{:S(2)}, u32[]{:S(2)}) collective-permute-start(f32[1,4,32]{2,1,0:T(4,128)S(1)} %get-tuple-element.47), channel_id=1, source_target_pairs={{16,0},{32,16},{48,32},{64,48},{80,64},{96,80},{112,96},{128,112},... | collective-permute-start | bytes 1544 | tf_op jit(solution)/shard_map/ppermute | solution.py:29
  142.1 85.0 %copy-start.4 = (f32[8,8,64]{2,1,0:T(8,128)}, f32[8,8,64]{2,1,0:T(8,128)S(1)}, u32[]{:S(2)}) copy-start(f32[8,8,64]{2,1,0:T(8,128)S(1)} %fusion.73) | copy-start | bytes 49156
  142.1 14.6 %collective-permute-start.21 = (f32[1,8,64]{2,1,0:T(8,128)S(1)}, f32[1,8,64]{2,1,0:T(8,128)S(1)}, u32[]{:S(2)}, u32[]{:S(2)}) collective-permute-start(f32[1,8,64]{2,1,0:T(8,128)S(1)} %get-tuple-element.28), channel_id=1, source_target_pairs={{0,16},{16,32},{32,48},{48,64},{64,80},{80,96},{96,112},{112,128},... | collective-permute-start | bytes 6152 | tf_op jit(solution)/shard_map/ppermute | solution.py:27
  147.4 9.3 %collective-permute-start.20 = (f32[1,8,64]{2,1,0:T(8,128)S(1)}, f32[1,8,64]{2,1,0:T(8,128)S(1)}, u32[]{:S(2)}, u32[]{:S(2)}) collective-permute-start(f32[1,8,64]{2,1,0:T(8,128)S(1)} %get-tuple-element.29), channel_id=1, source_target_pairs={{16,0},{32,16},{48,32},{64,48},{80,64},{96,80},{112,96},{128,112},... | collective-permute-start | bytes 6152 | tf_op jit(solution)/shard_map/ppermute | solution.py:29
  149.3 14.4 %collective-permute-start.27 = (f32[6,1,32]{2,1,0:T(1,128)S(1)}, f32[6,1,32]{2,1,0:T(1,128)S(1)}, u32[]{:S(2)}, u32[]{:S(2)}) collective-permute-start(f32[6,1,32]{2,1,0:T(1,128)S(1)} %get-tuple-element.40), channel_id=1, source_target_pairs={{0,1},{1,2},{2,3},{3,4},{4,5},{5,6},{6,7},{7,8},{8,9},{9,10},{10,1... | collective-permute-start | bytes 2312 | tf_op jit(solution)/shard_map/ppermute | solution.py:27
  154.8 9.0 %collective-permute-start.26 = (f32[6,1,32]{2,1,0:T(1,128)S(1)}, f32[6,1,32]{2,1,0:T(1,128)S(1)}, u32[]{:S(2)}, u32[]{:S(2)}) collective-permute-start(f32[6,1,32]{2,1,0:T(1,128)S(1)} %get-tuple-element.41), channel_id=1, source_target_pairs={{1,0},{2,1},{3,2},{4,3},{5,4},{6,5},{7,6},{8,7},{9,8},{10,9},{11,1... | collective-permute-start | bytes 2312 | tf_op jit(solution)/shard_map/ppermute | solution.py:29
  156.7 8.4 %collective-permute-start.23 = (f32[10,1,64]{2,1,0:T(1,128)S(1)}, f32[10,1,64]{2,1,0:T(1,128)S(1)}, u32[]{:S(2)}, u32[]{:S(2)}) collective-permute-start(f32[10,1,64]{2,1,0:T(1,128)S(1)} %get-tuple-element.22), channel_id=1, source_target_pairs={{0,1},{1,2},{2,3},{3,4},{4,5},{5,6},{6,7},{7,8},{8,9},{9,10},{10,1... | collective-permute-start | bytes 7688 | tf_op jit(solution)/shard_map/ppermute | solution.py:27
  161.6 6.1 %collective-permute-start.22 = (f32[10,1,64]{2,1,0:T(1,128)S(1)}, f32[10,1,64]{2,1,0:T(1,128)S(1)}, u32[]{:S(2)}, u32[]{:S(2)}) collective-permute-start(f32[10,1,64]{2,1,0:T(1,128)S(1)} %get-tuple-element.23), channel_id=1, source_target_pairs={{1,0},{2,1},{3,2},{4,3},{5,4},{6,5},{7,6},{8,7},{9,8},{10,9},{11,1... | collective-permute-start | bytes 7688 | tf_op jit(solution)/shard_map/ppermute | solution.py:29
  169.3 8.9 %collective-permute-start.29 = (f32[1,4,32]{2,1,0:T(4,128)S(1)}, f32[1,4,32]{2,1,0:T(4,128)S(1)}, u32[]{:S(2)}, u32[]{:S(2)}) collective-permute-start(f32[1,4,32]{2,1,0:T(4,128)S(1)} %get-tuple-element.44), channel_id=1, source_target_pairs={{0,16},{16,32},{32,48},{48,64},{64,80},{80,96},{96,112},{112,128},... | collective-permute-start | bytes 1544 | tf_op jit(solution)/shard_map/ppermute | solution.py:27
  176.3 7.6 %collective-permute-start.28 = (f32[1,4,32]{2,1,0:T(4,128)S(1)}, f32[1,4,32]{2,1,0:T(4,128)S(1)}, u32[]{:S(2)}, u32[]{:S(2)}) collective-permute-start(f32[1,4,32]{2,1,0:T(4,128)S(1)} %get-tuple-element.45), channel_id=1, source_target_pairs={{16,0},{32,16},{48,32},{64,48},{80,64},{96,80},{112,96},{128,112},... | collective-permute-start | bytes 1544 | tf_op jit(solution)/shard_map/ppermute | solution.py:29
  183.9 5.6 %collective-permute-start.31 = (f32[6,1,32]{2,1,0:T(1,128)S(1)}, f32[6,1,32]{2,1,0:T(1,128)S(1)}, u32[]{:S(2)}, u32[]{:S(2)}) collective-permute-start(f32[6,1,32]{2,1,0:T(1,128)S(1)} %get-tuple-element.38), channel_id=1, source_target_pairs={{0,1},{1,2},{2,3},{3,4},{4,5},{5,6},{6,7},{7,8},{8,9},{9,10},{10,1... | collective-permute-start | bytes 2312 | tf_op jit(solution)/shard_map/ppermute | solution.py:27
  187.6 6.1 %collective-permute-start.30 = (f32[6,1,32]{2,1,0:T(1,128)S(1)}, f32[6,1,32]{2,1,0:T(1,128)S(1)}, u32[]{:S(2)}, u32[]{:S(2)}) collective-permute-start(f32[6,1,32]{2,1,0:T(1,128)S(1)} %get-tuple-element.39), channel_id=1, source_target_pairs={{1,0},{2,1},{3,2},{4,3},{5,4},{6,5},{7,6},{8,7},{9,8},{10,9},{11,1... | collective-permute-start | bytes 2312 | tf_op jit(solution)/shard_map/ppermute | solution.py:29
  193.9 33.3 %copy-start.5 = (f32[4,4,32]{2,1,0:T(4,128)}, f32[4,4,32]{2,1,0:T(4,128)S(1)}, u32[]{:S(2)}) copy-start(f32[4,4,32]{2,1,0:T(4,128)S(1)} %add_add_fusion.2) | copy-start | bytes 6148
  193.9 5.3 %collective-permute-start.33 = (f32[1,4,32]{2,1,0:T(4,128)S(1)}, f32[1,4,32]{2,1,0:T(4,128)S(1)}, u32[]{:S(2)}, u32[]{:S(2)}) collective-permute-start(f32[1,4,32]{2,1,0:T(4,128)S(1)} %get-tuple-element.42), channel_id=1, source_target_pairs={{0,16},{16,32},{32,48},{48,64},{64,80},{80,96},{96,112},{112,128},... | collective-permute-start | bytes 1544 | tf_op jit(solution)/shard_map/ppermute | solution.py:27
  195.8 7.6 %collective-permute-start.32 = (f32[1,4,32]{2,1,0:T(4,128)S(1)}, f32[1,4,32]{2,1,0:T(4,128)S(1)}, u32[]{:S(2)}, u32[]{:S(2)}) collective-permute-start(f32[1,4,32]{2,1,0:T(4,128)S(1)} %get-tuple-element.43), channel_id=1, source_target_pairs={{16,0},{32,16},{48,32},{64,48},{80,64},{96,80},{112,96},{128,112},... | collective-permute-start | bytes 1544 | tf_op jit(solution)/shard_map/ppermute | solution.py:29
  203.5 5.0 %collective-permute-start.35 = (f32[6,1,32]{2,1,0:T(1,128)S(1)}, f32[6,1,32]{2,1,0:T(1,128)S(1)}, u32[]{:S(2)}, u32[]{:S(2)}) collective-permute-start(f32[6,1,32]{2,1,0:T(1,128)S(1)} %get-tuple-element.36), channel_id=1, source_target_pairs={{0,1},{1,2},{2,3},{3,4},{4,5},{5,6},{6,7},{7,8},{8,9},{9,10},{10,1... | collective-permute-start | bytes 2312 | tf_op jit(solution)/shard_map/ppermute | solution.py:27
  206.6 6.1 %collective-permute-start.34 = (f32[6,1,32]{2,1,0:T(1,128)S(1)}, f32[6,1,32]{2,1,0:T(1,128)S(1)}, u32[]{:S(2)}, u32[]{:S(2)}) collective-permute-start(f32[6,1,32]{2,1,0:T(1,128)S(1)} %get-tuple-element.37), channel_id=1, source_target_pairs={{1,0},{2,1},{3,2},{4,3},{5,4},{6,5},{7,6},{8,7},{9,8},{10,9},{11,1... | collective-permute-start | bytes 2312 | tf_op jit(solution)/shard_map/ppermute | solution.py:29
where the time goes:
time: 228 us; the launch traced here: 227 us
  starting transfers between devices  121 us (53%)
  waiting for transfers between devices  40.2 us (18%)
  local copies, waits for them, and re-layouts  35.9 us (16%)
  other arithmetic  15.5 us (7%)
  blocking collectives  13.3 us (6%)
    ppermute x18, starting transfers between devices, with_halo(): lax.ppermute(tail, axis, [(i, (i + 1) % count) for i in range(ends)])  80.1 us
    ppermute x18, starting transfers between devices, with_halo(): lax.ppermute(head, axis, [((i + 1) % count, i) for i in range(ends)])  40.6 us
    ppermute x18, waiting for transfers between devices, with_halo(): lax.ppermute(head, axis, [((i + 1) % count, i) for i in range(ends)])  40.2 us
    reshape x5, local copies, waits for them, and re-layouts, restrict(): field.reshape(field.shape[0] // 2, 2, field.shape[1] // 2, 2, field.shape...  31.4 us
    all_gather x1, blocking collectives, body(): coarse_rhs = lax.all_gather(source, 'group', axis=1, tiled=True)  13.3 us
    reduce_sum x7, other arithmetic, restrict(): return shaped.mean(axis=(1, 3, 5))  12.6 us
  transfers between devices with their start and end apart: 36, of which 9 were waited for; matrix products, arithmetic and copies ran while one was open for 14% of the time, Pallas kernels for 0%

commit v1 on v0

v1 whole, which is shorter than its diff:
```python
import functools

import jax
import jax.numpy as jnp
from jax import lax
from jax.experimental import pallas as pl
from jax.experimental.pallas import tpu as pltpu
from jax.sharding import PartitionSpec as P

MESH = pl.DeviceIdType.MESH

center_value = 1.1
half_width = 0.8
ratio_sigma = center_value / half_width
first_rho = 1.0 / ratio_sigma
second_rho = 1.0 / (2.0 * ratio_sigma - first_rho)
carry_factor = second_rho * first_rho
push_factor = 2.0 * second_rho / half_width

alpha = (1.0 + carry_factor) / center_value + push_factor * (1.0 - 1.0 / center_value)
beta = push_factor / center_value

OUTSIDE_MASS = 1e30
LANES = 128
I0, J0, W0, E0 = 3, 8, 16, (22, 32, LANES)
I1, W1, E1 = 8, 8, (24, 24, LANES)

DIRS = [(1, 0), (-1, 0), (1, 1), (1, -1), (-1, 1), (-1, -1), (0, 1), (0, -1)]


def cut(step, start, size, width):
    if step == 0:
        return start, start, size
    if step > 0:
        return start + size - width, start - width, width
    return start, start + size, width


def lane_shift(a, by, lane):
    low = jnp.where(lane >= by, pltpu.roll(a, by, axis=2), 0.0)
    high = jnp.where(lane < LANES - by, pltpu.roll(a, LANES - by, axis=2), 0.0)
    return low + high


def around(a, by):
    mid = a[1:-1]
    cols = a.shape[1]
    lane = lax.broadcasted_iota(jnp.int32, mid.shape, 2)
    total = a[2:] + a[:-2]
    total = total + pltpu.roll(mid, 1, axis=1) + pltpu.roll(mid, cols - 1, axis=1)
    return total + lane_shift(mid, by, lane)


def spread(u, c, by):
    return c[1:-1] * around(u, by) + around(c * u, by)


def inverse(m, c, by):
    diag = m[1:-1] + 6.0 * c[1:-1] + around(c, by)
    rough = pl.reciprocal(diag, approx=True)
    rough = rough * (2.0 - diag * rough)
    return rough * (2.0 - diag * rough)


def smooth(f, c, invd, by):
    s = beta * spread(f * invd, c, by)
    x2 = invd[1:-1] * (alpha * f[1:-1] + s)
    r2 = (1.0 - alpha) * f[2:-2] - s[1:-1] + spread(x2, c[1:-1], by)
    return x2, r2


def pool(a, scratch, by):
    rows, cols, _ = a.shape
    pair = a.reshape(rows // 2, 2, cols, LANES)
    scratch[0 : rows // 2, 0:cols, :] = pair[:, 0] + pair[:, 1]
    even = scratch[0 : rows // 2, pl.ds(0, cols // 2, stride=2), :]
    odd = scratch[0 : rows // 2, pl.ds(1, cols // 2, stride=2), :]
    both = even + odd
    return 0.125 * (both + pltpu.roll(both, LANES - by, axis=2))


def squeeze(a, by):
    shape = (LANES, LANES // by)
    pick = lax.broadcasted_iota(jnp.int32, shape, 0) == by * lax.broadcasted_iota(jnp.int32, shape, 1)
    return lax.dot(
        a, pick.astype(jnp.float32), precision=lax.Precision.HIGHEST, preferred_element_type=jnp.float32
    )


def main_kernel(
    bricks, groups,
    f_ref, m_ref, c_ref,
    fine_ref, middle_ref, coarse_ref, gather_ref,
    x0, x1, f1, pool0, pool1, pool2, f3,
    fine_buf, middle_buf, coarse_buf,
    load_sem, out_sem, send_a, recv_a, send_b, recv_b, send_c, recv_c, send_d, recv_d,
):
    b, g = lax.axis_index("brick"), lax.axis_index("group")

    loads = [
        pltpu.make_async_copy(ref, x0.at[i, pl.ds(I0, W0), pl.ds(J0, W0), :], load_sem.at[i])
        for i, ref in enumerate((f_ref, m_ref, c_ref))
    ]
    for copy in loads:
        copy.start()

    barrier = pltpu.get_barrier_semaphore()

    def reach(step):
        db, dg = step
        ok = (b + db >= 0) & (b + db < bricks) & (g + dg >= 0) & (g + dg < groups)
        return ok, {"brick": b + db, "group": g + dg}

    expected = groups - 1
    for step in DIRS[:6]:
        ok, peer = reach(step)
        expected = expected + ok.astype(jnp.int32)

        @pl.when(ok)
        def _():
            pl.semaphore_signal(barrier, inc=1, device_id=peer, device_id_type=MESH)

    def mate(k):
        return {"brick": b, "group": lax.rem(g + k, groups)}

    for k in range(1, groups):
        pl.semaphore_signal(barrier, inc=1, device_id=mate(k), device_id_type=MESH)

    def blank(rows0, cols0, rows1, cols1):
        for ref, rows, cols in ((x0, rows0, cols0), (x1, rows1, cols1)):
            shape = (rows.size, cols.size, LANES)
            if ref is x0:
                ref[0, rows, cols, :] = jnp.zeros(shape, jnp.float32)
                ref[1, rows, cols, :] = jnp.full(shape, OUTSIDE_MASS, jnp.float32)
                ref[2, rows, cols, :] = jnp.zeros(shape, jnp.float32)
            else:
                ref[0, rows, cols, :] = jnp.full(shape, OUTSIDE_MASS, jnp.float32)
                ref[1, rows, cols, :] = jnp.zeros(shape, jnp.float32)
                f1[rows, cols, :] = jnp.zeros(shape, jnp.float32)

    every0, every1 = pl.ds(0, E0[1]), pl.ds(0, E1[1])

    @pl.when(b == 0)
    def _():
        blank(pl.ds(0, I0), every0, pl.ds(0, I1), every1)

    @pl.when(b == bricks - 1)
    def _():
        blank(pl.ds(I0 + W0, I0), every0, pl.ds(I1 + W1, I1), every1)

    @pl.when(g == 0)
    def _():
        blank(pl.ds(0, E0[0]), pl.ds(0, J0), pl.ds(0, E1[0]), pl.ds(0, I1))

    @pl.when(g == groups - 1)
    def _():
        blank(pl.ds(0, E0[0]), pl.ds(J0 + W0, J0), pl.ds(0, E1[0]), pl.ds(I1 + W1, I1))

    for copy in loads:
        copy.wait()
    own0 = (pl.ds(I0, W0), pl.ds(J0, W0))
    own1 = (pl.ds(I1, W1), pl.ds(I1, W1))
    x1[(0, *own1)] = pool(x0[(1, *own0)], pool0, 1)
    x1[(1, *own1)] = pool(x0[(2, *own0)], pool0, 1)

    pl.semaphore_wait(barrier, expected)

    def message(ref, lead, step, widths, at, sizes, send, recv, peer):
        si, ti, ni = cut(step[0], at[0], sizes[0], widths[0])
        sj, tj, nj = cut(step[1], at[1], sizes[1], widths[1])
        return pltpu.make_async_remote_copy(
            src_ref=ref.at[(*lead, pl.ds(si, ni), pl.ds(sj, nj))],
            dst_ref=ref.at[(*lead, pl.ds(ti, ni), pl.ds(tj, nj))],
            send_sem=send, recv_sem=recv, device_id=peer, device_id_type=MESH,
        )

    def stage_a(i, step, peer):
        at, sizes = (I0, J0), (W0, W0)
        if step[0] and step[1]:
            return [message(x0, (pl.ds(0, 3),), step, (2, 2), at, sizes, send_a.at[i, 0], recv_a.at[i, 0], peer)]
        return [
            message(x0, (pl.ds(0, 2),), step, (2, 2), at, sizes, send_a.at[i, 0], recv_a.at[i, 0], peer),
            message(x0, (2,), step, (3, 3), at, sizes, send_a.at[i, 1], recv_a.at[i, 1], peer),
        ]

    def stage_b(i, step, peer):
        rows = 6 if step[1] else 7
        return [message(x1, (pl.ds(0, 2),), step, (rows, W1), (I1, I1), (W1, W1), send_b.at[i], recv_b.at[i], peer)]

    def stage_c(i, step, peer):
        rows = 5 if step[1] else 6
        return [message(f1, (), step, (rows, W1), (I1, I1), (W1, W1), send_c.at[i], recv_c.at[i], peer)]

    def each(stage, act):
        for i, step in enumerate(DIRS):
            ok, peer = reach(step)

            @pl.when(ok)
            def _():
                for copy in stage(i, step, peer):
                    act(copy)

    def receive(stage):
        for i, step in enumerate(DIRS):
            ok, peer = reach((-step[0], -step[1]))

            @pl.when(ok)
            def _():
                for copy in stage(i, step, peer):
                    copy.wait_recv()

    each(stage_a, lambda copy: copy.start())
    each(stage_b, lambda copy: copy.start())

    receive(stage_a)
    f, m, c = x0[0], x0[1], 0.125 * x0[2]
    invd = inverse(m, c, 1)
    x2, r2 = smooth(f[1:-1], c[1:-1], invd, 1)
    fine_buf[...] = x2[1:-1, J0 : J0 + W0]
    f1[own1] = pool(r2[:, J0 : J0 + W0], pool0, 1)
    each(stage_c, lambda copy: copy.start())
    fine_out = pltpu.make_async_copy(fine_buf, fine_ref, out_sem.at[0])
    fine_out.start()

    receive(stage_b)
    m1, c1 = x1[0], x1[1]
    c2 = 0.125 * pool(c1, pool1, 2)
    m2 = pool(m1, pool1, 2)
    c1 = 0.125 * c1
    invd1 = inverse(m1, c1, 2)
    invd2 = inverse(m2, c2, 4)

    receive(stage_c)
    x2, r2 = smooth(f1[2:22], c1[2:22], invd1[1:21], 2)
    middle = x2[5:13, I1 : I1 + W1]
    f2 = pool(r2, pool1, 2)
    x2, r2 = smooth(f2, c2[2:10], invd2[1:9], 4)
    coarse = x2[1:5, 4:8]
    pool2[...] = jnp.stack([r2[0] + r2[1], r2[2] + r2[3]])
    both = pool2[:, pl.ds(4, 2, stride=2), :] + pool2[:, pl.ds(5, 2, stride=2), :]
    f3[...] = 0.125 * (both + pltpu.roll(both, LANES - 4, axis=2))

    keep = pltpu.make_async_copy(f3, gather_ref.at[:, g], out_sem.at[1])
    keep.start()

    def share(k):
        return pltpu.make_async_remote_copy(
            src_ref=f3, dst_ref=gather_ref.at[:, g], send_sem=send_d.at[k], recv_sem=recv_d.at[k],
            device_id=mate(k), device_id_type=MESH,
        )

    def shared(k):
        owner = lax.rem(g + groups - k, groups)
        return pltpu.make_async_remote_copy(
            src_ref=f3, dst_ref=gather_ref.at[:, owner], send_sem=send_d.at[k], recv_sem=recv_d.at[k],
            device_id=mate(k), device_id_type=MESH,
        )

    for k in range(1, groups):
        share(k).start()

    middle_buf[...] = squeeze(middle.reshape(W1 * W1, LANES), 2).reshape(W1, W1, LANES // 2)
    for i in range(4):
        coarse_buf[i] = squeeze(coarse[i], 4)
    outs = [
        pltpu.make_async_copy(middle_buf, middle_ref, out_sem.at[2]),
        pltpu.make_async_copy(coarse_buf, coarse_ref, out_sem.at[3]),
    ]
    for copy in outs:
        copy.start()

    for k in range(1, groups):
        shared(k).wait_recv()
    for copy in (fine_out, keep, *outs):
        copy.wait()
    each(stage_a, lambda copy: copy.wait_send())
    each(stage_b, lambda copy: copy.wait_send())
    each(stage_c, lambda copy: copy.wait_send())
    for k in range(1, groups):
        share(k).wait_send()


def finish_kernel(fine, middle, coarse, gathered, fine_out, middle_out, coarse_out, rhs_out):
    fine_out[...] = fine[...]
    middle_out[...] = middle[...]
    coarse_out[...] = coarse[...]
    depth = rhs_out.shape[1]
    shape = (depth, LANES)
    pick = 8 * lax.broadcasted_iota(jnp.int32, shape, 0) == lax.broadcasted_iota(jnp.int32, shape, 1)
    for i in range(2):
        rhs_out[i] = lax.dot_general(
            pick.astype(jnp.float32), gathered[i], (((1,), (1,)), ((), ())),
            precision=lax.Precision.HIGHEST, preferred_element_type=jnp.float32,
        )


def solution(mesh):
    bricks, groups = mesh.shape["brick"], mesh.shape["group"]
    anywhere = pl.BlockSpec(memory_space=pl.ANY)
    vmem = pl.BlockSpec(memory_space=pltpu.VMEM)

    def f32(*shape):
        return jax.ShapeDtypeStruct(shape, jnp.float32)

    def buf(*shape):
        return pltpu.VMEM(shape, jnp.float32)

    dma = pltpu.SemaphoreType.DMA

    def body(right_side, mass_coef, face_coef):
        small = (f32(W0, W0, LANES), f32(W1, W1, LANES // 2), f32(4, 4, LANES // 4))
        fine, middle, coarse, gathered = pl.pallas_call(
            functools.partial(main_kernel, bricks, groups),
            out_shape=(*small, f32(2, groups, 2, LANES)),
            in_specs=[anywhere] * 3,
            out_specs=(anywhere,) * 4,
            scratch_shapes=[
                buf(3, *E0), buf(2, *E1), buf(*E1),
                buf(8, 16, LANES), buf(12, 24, LANES), buf(2, 12, LANES), buf(2, 2, LANES),
                buf(W0, W0, LANES), buf(W1, W1, LANES // 2), buf(4, 4, LANES // 4),
                dma((3,)), dma((4,)), dma((8, 2)), dma((8, 2)), dma((8,)), dma((8,)), dma((8,)), dma((8,)),
                dma((groups,)), dma((groups,)),
            ],
            compiler_params=pltpu.CompilerParams(
                collective_id=0, has_side_effects=True, vmem_limit_bytes=32 * 1024 * 1024
            ),
            name="cycle",
        )(right_side, mass_coef, face_coef)
        fine, middle, coarse, rhs = pl.pallas_call(
            finish_kernel,
            out_shape=(*small, f32(2, LANES // 8, 2 * groups)),
            in_specs=[vmem] * 4,
            out_specs=(vmem,) * 4,
            name="finish",
        )(fine, middle, coarse, gathered.reshape(2, 2 * groups, LANES))
        return fine, middle, coarse, jnp.swapaxes(rhs, 1, 2)

    placed = P("brick", "group", None)
    return jax.shard_map(
        body,
        mesh=mesh,
        in_specs=(placed, placed, placed),
        out_specs=(placed, placed, placed, P("brick", None, None)),
        check_vma=False,
    )
```

time: 228 us -> 34.1 us (0.15)
  the two profiles are of different devices: /device:TPU:223 before, /device:TPU:199 now
where the time goes in v1:
time: 34.1 us; the launch traced here: 33.9 us
  Pallas kernels  28.1 us (82%)
  local copies, waits for them, and re-layouts  5.16 us (15%)
  between operations  0.66 us (2%)
    pallas_call x1, Pallas kernels, body(): pl.pallas_call(functools.partial(main_kernel, bricks, groups), out_shape=...  26.4 us
    unnamed x14, local copies, waits for them, and re-layouts  5.16 us
    pallas_call x1, Pallas kernels, body(): pl.pallas_call(finish_kernel, out_shape=(*small, f32(2, LANES // 8, 2 * g...  1.7 us

profile of v1, /device:TPU:199, one launch (start us, length us, event | category | flops | bytes accessed | tf_op | source)
XLA Modules:
  0.0 33.9 jit_solution(10596570120499388902)
XLA Ops:
  0.6 0.0 copy-start
  0.6 0.9 %copy-done = f32[16,16,128]{2,1,0:T(8,128)S(1)} copy-done((f32[16,16,128]{2,1,0:T(8,128)S(1)}, f32[16,16,128]{2,1,0:T(8,128)}, u32[]{:S(2)}) %copy-start) | copy-done | bytes 131096
  1.5 0.0 copy-start.1
  1.5 0.9 %copy-done.1 = f32[16,16,128]{2,1,0:T(8,128)S(1)} copy-done((f32[16,16,128]{2,1,0:T(8,128)S(1)}, f32[16,16,128]{2,1,0:T(8,128)}, u32[]{:S(2)}) %copy-start.1) | copy-done | bytes 131096
  2.4 0.0 copy-start.2
  2.4 0.9 %copy-done.2 = f32[16,16,128]{2,1,0:T(8,128)S(1)} copy-done((f32[16,16,128]{2,1,0:T(8,128)S(1)}, f32[16,16,128]{2,1,0:T(8,128)}, u32[]{:S(2)}) %copy-start.2) | copy-done | bytes 131096
  3.3 26.4 %cycle.1 = (f32[16,16,128]{2,1,0:T(8,128)S(1)}, f32[8,8,64]{2,1,0:T(8,128)S(1)}, f32[4,4,32]{2,1,0:T(4,128)S(1)}, f32[2,16,2,128]{3,2,1,0:T(2,128)S(1)}) custom-call(f32[16,16,128]{2,1,0:T(8,128)S(1)} %copy-done, f32[16,16,128]{2,1,0:T(8,128)S(1)} %copy-done.1, f32[16,16,128]{2,1,0:T(8,128)S(1)} %copy-done.2), custom_call_target="tpu_custom_call" | custom-call | tf_op jit(solution)/shard_map/cycle/pallas_call | solution.py:312
  29.7 0.0 copy-start.3
  29.7 0.6 %copy-done.3 = f32[16,16,128]{2,1,0:T(8,128)} copy-done((f32[16,16,128]{2,1,0:T(8,128)}, f32[16,16,128]{2,1,0:T(8,128)S(1)}, u32[]{:S(2)}) %copy-start.3) | copy-done | bytes 131096
  30.4 0.0 copy-start.4
  30.4 0.6 %copy-done.4 = f32[8,8,64]{2,1,0:T(8,128)} copy-done((f32[8,8,64]{2,1,0:T(8,128)}, f32[8,8,64]{2,1,0:T(8,128)S(1)}, u32[]{:S(2)}) %copy-start.4) | copy-done | bytes 16408
  31.0 0.0 copy-start.5
  31.0 0.6 %copy-done.5 = f32[2,16,2,128]{3,2,1,0:T(2,128)} copy-done((f32[2,16,2,128]{3,2,1,0:T(2,128)}, f32[2,16,2,128]{3,2,1,0:T(2,128)S(1)}, u32[]{:S(2)}) %copy-start.5) | copy-done | bytes 32792
  31.6 0.0 copy-start.6
  31.6 0.6 %copy-done.6 = f32[4,4,32]{2,1,0:T(4,128)} copy-done((f32[4,4,32]{2,1,0:T(4,128)}, f32[4,4,32]{2,1,0:T(4,128)S(1)}, u32[]{:S(2)}) %copy-start.6) | copy-done | bytes 2072
  32.2 1.7 %finish.1 = (f32[16,16,128]{2,1,0:T(8,128)}, f32[8,8,64]{2,1,0:T(8,128)}, f32[4,4,32]{2,1,0:T(4,128)}, f32[2,16,32]{2,1,0:T(8,128)}) custom-call(f32[16,16,128]{2,1,0:T(8,128)} %copy-done.3, f32[8,8,64]{2,1,0:T(8,128)} %copy-done.4, f32[4,4,32]{2,1,0:T(4,128)} %copy-done.6, f32[2,32,128]{2,1,0:T(8,128)} %bitcast.2), custom_call_target="tpu_custom_call" | custom-call | tf_op jit(solution)/shard_map/finish/pallas_call | solution.py:329
Async XLA Ops:
  0.6 0.9 %copy-start = (f32[16,16,128]{2,1,0:T(8,128)S(1)}, f32[16,16,128]{2,1,0:T(8,128)}, u32[]{:S(2)}) copy-start(f32[16,16,128]{2,1,0:T(8,128)} %f_ref.1) | copy-start | bytes 393220
  1.5 0.9 %copy-start.1 = (f32[16,16,128]{2,1,0:T(8,128)S(1)}, f32[16,16,128]{2,1,0:T(8,128)}, u32[]{:S(2)}) copy-start(f32[16,16,128]{2,1,0:T(8,128)} %m_ref.1) | copy-start | bytes 393220
  2.4 0.9 %copy-start.2 = (f32[16,16,128]{2,1,0:T(8,128)S(1)}, f32[16,16,128]{2,1,0:T(8,128)}, u32[]{:S(2)}) copy-start(f32[16,16,128]{2,1,0:T(8,128)} %c_ref.1) | copy-start | bytes 393220
  29.7 0.7 %copy-start.3 = (f32[16,16,128]{2,1,0:T(8,128)}, f32[16,16,128]{2,1,0:T(8,128)S(1)}, u32[]{:S(2)}) copy-start(f32[16,16,128]{2,1,0:T(8,128)S(1)} %get-tuple-element.12.fine) | copy-start | bytes 393220
  30.4 0.6 %copy-start.4 = (f32[8,8,64]{2,1,0:T(8,128)}, f32[8,8,64]{2,1,0:T(8,128)S(1)}, u32[]{:S(2)}) copy-start(f32[8,8,64]{2,1,0:T(8,128)S(1)} %get-tuple-element.13.middle) | copy-start | bytes 49156
  31.0 0.6 %copy-start.5 = (f32[2,16,2,128]{3,2,1,0:T(2,128)}, f32[2,16,2,128]{3,2,1,0:T(2,128)S(1)}, u32[]{:S(2)}) copy-start(f32[2,16,2,128]{3,2,1,0:T(2,128)S(1)} %get-tuple-element.15) | copy-start | bytes 98308
  31.6 0.6 %copy-start.6 = (f32[4,4,32]{2,1,0:T(4,128)}, f32[4,4,32]{2,1,0:T(4,128)S(1)}, u32[]{:S(2)}) copy-start(f32[4,4,32]{2,1,0:T(4,128)S(1)} %get-tuple-element.14.coarse) | copy-start | bytes 6148

commit v2 on v1

v2 whole, which is shorter than its diff:
```python
import functools

import jax
import jax.numpy as jnp
from jax import lax
from jax.experimental import pallas as pl
from jax.experimental.pallas import tpu as pltpu
from jax.sharding import PartitionSpec as P

MESH = pl.DeviceIdType.MESH

center_value = 1.1
half_width = 0.8
ratio_sigma = center_value / half_width
first_rho = 1.0 / ratio_sigma
second_rho = 1.0 / (2.0 * ratio_sigma - first_rho)
carry_factor = second_rho * first_rho
push_factor = 2.0 * second_rho / half_width

alpha = (1.0 + carry_factor) / center_value + push_factor * (1.0 - 1.0 / center_value)
beta = push_factor / center_value

OUTSIDE_MASS = 1e30
LANES = 128
I0, J0, W0, E0 = 3, 8, 16, (22, 32, LANES)
I1, H1, J1, W1, E1 = 4, 4, 8, 8, (12, 24, LANES)

DIRS = [(1, 0), (-1, 0), (1, 1), (1, -1), (-1, 1), (-1, -1), (0, 1), (0, -1)]


def cut(step, start, size, width):
    if step == 0:
        return start, start, size
    if step > 0:
        return start + size - width, start - width, width
    return start, start + size, width


def lanes_of(a):
    return lax.broadcasted_iota(jnp.int32, a.shape, a.ndim - 1)


def turn(a, by):
    return pltpu.roll(a, by % LANES, axis=a.ndim - 1)


def beside(mid, by):
    lane = lanes_of(mid)
    low = jnp.where(lane >= by, turn(mid, by), 0.0)
    high = jnp.where(lane < LANES - by, turn(mid, -by), 0.0)
    cols = mid.shape[1]
    return low + high + pltpu.roll(mid, 1, axis=1) + pltpu.roll(mid, cols - 1, axis=1)


def around(a, by):
    return a[2:] + a[:-2] + beside(a[1:-1], by)


def around_pairs(a, by):
    up, down = turn(a[:-1], -1), turn(a[1:], 1)
    even = lanes_of(a[1:-1]) % 2 == 0
    return jnp.where(even, up[1:] + up[:-1], down[1:] + down[:-1]) + beside(a[1:-1], by)


def inverse(m, c, total):
    diag = m + 0.75 * c + 0.125 * total
    rough = pl.reciprocal(diag, approx=True)
    rough = rough * (2.0 - diag * rough)
    return rough * (2.0 - diag * rough)


def squeeze(a, by, first=0):
    shape = (LANES, LANES // by)
    pick = lax.broadcasted_iota(jnp.int32, shape, 0) == by * lax.broadcasted_iota(jnp.int32, shape, 1) + first
    return lax.dot(
        a, pick.astype(jnp.float32), precision=lax.Precision.HIGHEST, preferred_element_type=jnp.float32
    )


def halve(a, scratch):
    rows, cols, _ = a.shape
    scratch[0:rows, 0:cols, :] = a
    return scratch[0:rows, pl.ds(0, cols // 2, stride=2), :] + scratch[0:rows, pl.ds(1, cols // 2, stride=2), :]


def pack_pool(a, scratch):
    rows, cols, _ = a.shape
    quad = a.reshape(rows // 4, 4, cols, LANES)
    upper, lower = halve(quad[:, 0] + quad[:, 1], scratch.at[0]), halve(quad[:, 2] + quad[:, 3], scratch.at[1])
    even = lanes_of(upper) % 2 == 0
    return 0.125 * jnp.where(even, upper + turn(upper, -1), lower + turn(lower, 1))


def unpack_pool(a, scratch):
    both = halve(a, scratch)
    both = both + turn(both, -1)
    return 0.125 * (both + turn(both, -2))


def main_kernel(
    bricks, groups,
    f_ref, m_ref, c_ref,
    fine_ref, middle_ref, coarse_ref, gather_ref,
    x0, x1, f1, inv0, y0, cy0, x20, cx20, base0, r0, pool0, pool1, pool2, f3,
    load_sem, send_a, recv_a, send_b, recv_b, send_c, recv_c, send_d, recv_d,
):
    b, g = lax.axis_index("brick"), lax.axis_index("group")
    barrier = pltpu.get_barrier_semaphore()

    def reach(step):
        db, dg = step
        ok = (b + db >= 0) & (b + db < bricks) & (g + dg >= 0) & (g + dg < groups)
        return ok, {"brick": b + db, "group": g + dg}

    def mate(k):
        return {"brick": b, "group": lax.rem(g + k, groups)}

    mates = sorted(range(1, groups), key=lambda k: (abs(2 * k - groups), k))

    expected = groups - 1
    for step in DIRS[:6]:
        ok, peer = reach(step)
        expected = expected + ok.astype(jnp.int32)

        @pl.when(ok)
        def _():
            pl.semaphore_signal(barrier, inc=1, device_id=peer, device_id_type=MESH)

    for k in mates:
        pl.semaphore_signal(barrier, inc=1, device_id=mate(k), device_id_type=MESH)

    loads = [
        pltpu.make_async_copy(ref, x0.at[i, pl.ds(I0, W0), pl.ds(J0, W0), :], load_sem.at[i])
        for i, ref in enumerate((f_ref, m_ref, c_ref))
    ]
    for copy in loads:
        copy.start()

    def blank(rows0, cols0, rows1, cols1):
        shape0, shape1 = (rows0.size, cols0.size, LANES), (rows1.size, cols1.size, LANES)
        for i, value in enumerate((0.0, OUTSIDE_MASS, 0.0)):
            x0[i, rows0, cols0, :] = jnp.full(shape0, value, jnp.float32)
        for i, value in enumerate((OUTSIDE_MASS, 0.0)):
            x1[i, rows1, cols1, :] = jnp.full(shape1, value, jnp.float32)
        f1[rows1, cols1, :] = jnp.zeros(shape1, jnp.float32)

    every = (pl.ds(0, E0[0]), pl.ds(0, E0[1]), pl.ds(0, E1[0]), pl.ds(0, E1[1]))

    @pl.when(b == 0)
    def _():
        blank(pl.ds(0, I0), every[1], pl.ds(0, I1), every[3])

    @pl.when(b == bricks - 1)
    def _():
        blank(pl.ds(I0 + W0, I0), every[1], pl.ds(I1 + H1, I1), every[3])

    @pl.when(g == 0)
    def _():
        blank(every[0], pl.ds(0, J0), every[2], pl.ds(0, J1))

    @pl.when(g == groups - 1)
    def _():
        blank(every[0], pl.ds(J0 + W0, J0), every[2], pl.ds(J1 + W1, J1))

    for copy in loads:
        copy.wait()
    own0 = (pl.ds(I0, W0), pl.ds(J0, W0))
    own1 = (pl.ds(I1, H1), pl.ds(J1, W1))
    x1[(0, *own1)] = pack_pool(x0[(1, *own0)], pool0)
    x1[(1, *own1)] = pack_pool(x0[(2, *own0)], pool0)

    pl.semaphore_wait(barrier, expected)

    def message(ref, lead, step, widths, at, sizes, send, recv, peer):
        si, ti, ni = cut(step[0], at[0], sizes[0], widths[0])
        sj, tj, nj = cut(step[1], at[1], sizes[1], widths[1])
        return pltpu.make_async_remote_copy(
            src_ref=ref.at[(*lead, pl.ds(si, ni), pl.ds(sj, nj))],
            dst_ref=ref.at[(*lead, pl.ds(ti, ni), pl.ds(tj, nj))],
            send_sem=send, recv_sem=recv, device_id=peer, device_id_type=MESH,
        )

    def stage_a(i, step, peer):
        at, sizes = (I0, J0), (W0, W0)
        if step[0] and step[1]:
            return [message(x0, (pl.ds(0, 3),), step, (2, 2), at, sizes, send_a.at[i, 0], recv_a.at[i, 0], peer)]
        return [
            message(x0, (pl.ds(0, 2),), step, (2, 2), at, sizes, send_a.at[i, 0], recv_a.at[i, 0], peer),
            message(x0, (2,), step, (3, 3), at, sizes, send_a.at[i, 1], recv_a.at[i, 1], peer),
        ]

    def stage_b(i, step, peer):
        rows = 3 if step[1] else 4
        return [message(x1, (pl.ds(0, 2),), step, (rows, W1), (I1, J1), (H1, W1), send_b.at[i], recv_b.at[i], peer)]

    def stage_c(i, step, peer):
        return [message(f1, (), step, (3, W1), (I1, J1), (H1, W1), send_c.at[i], recv_c.at[i], peer)]

    def each(stage, act, keep=lambda step: True):
        for i, step in enumerate(DIRS):
            if keep(step):
                ok, peer = reach(step)

                @pl.when(ok)
                def _():
                    for copy in stage(i, step, peer):
                        act(copy)

    def receive(stage, keep=lambda step: True):
        for i, step in reversed(list(enumerate(DIRS))):
            if keep(step):
                ok, peer = reach((-step[0], -step[1]))

                @pl.when(ok)
                def _():
                    for copy in stage(i, step, peer):
                        copy.wait_recv()

    def start(copy):
        copy.start()

    each(stage_a, start)
    each(stage_b, start)

    def diagonal(a, z):
        f, m, c = x0[0, a:z], x0[1, a:z], x0[2, a - 1 : z + 1]
        invd = inverse(m, c[1:-1], around(c, 1))
        y = f * invd
        inv0[a:z], y0[a:z], cy0[a:z] = invd, y, c[1:-1] * y

    def second(a, z):
        f, c = x0[0, a:z], x0[2, a:z]
        s = (0.125 * beta) * (c * around(y0[a - 1 : z + 1], 1) + around(cy0[a - 1 : z + 1], 1))
        x2 = inv0[a:z] * (alpha * f + s)
        x20[a:z], cx20[a:z], base0[a:z] = x2, c * x2, (1.0 - alpha) * f - s

    def residual(a, z):
        c = x0[2, a:z]
        total = c * around(x20[a - 1 : z + 1], 1) + around(cx20[a - 1 : z + 1], 1)
        r0[a:z] = (base0[a:z] + 0.125 * total)[:, J0 : J0 + W0]

    receive(stage_a, lambda step: step[0] == 0)
    diagonal(4, 18)
    second(5, 17)
    residual(6, 16)
    receive(stage_a, lambda step: step[0] == 1)
    diagonal(1, 4)
    second(2, 5)
    residual(3, 6)
    receive(stage_a, lambda step: step[0] == -1)
    diagonal(18, 21)
    second(17, 20)
    residual(16, 19)
    f1[own1] = pack_pool(r0[I0 : I0 + W0], pool0)
    each(stage_c, start)
    fine_ref[...] = x20[(pl.ds(I0, W0), pl.ds(J0, W0))]

    receive(stage_b)
    m1, c1 = x1[0], x1[1]
    c2 = unpack_pool(c1, pool1)
    m2 = unpack_pool(m1, pool1)
    invd1 = inverse(m1[1:-1], c1[1:-1], around_pairs(c1, 2))
    invd2 = inverse(m2[1:-1], c2[1:-1], around(c2, 4))
    each(stage_a, lambda copy: copy.wait_send())
    each(stage_b, lambda copy: copy.wait_send())

    receive(stage_c)
    f = f1[1:-1]
    y = f * invd1
    edge = jnp.zeros((1, *E1[1:]), jnp.float32)
    y = jnp.concatenate([edge, y, edge], axis=0)
    s = (0.125 * beta) * (c1[1:-1] * around_pairs(y, 2) + around_pairs(c1 * y, 2))
    x2 = invd1 * (alpha * f + s)
    middle = x2[3:7, J1 : J1 + W1]
    cx2 = c1[1:-1] * x2
    total = c1[2:-2] * around_pairs(x2, 2) + around_pairs(cx2, 2)
    r2 = (1.0 - alpha) * f[1:-1] - s[1:-1] + 0.125 * total

    f = unpack_pool(r2, pool1)
    c, invd = c2[2:10], invd2[1:9]
    y = f * invd
    s = (0.125 * beta) * (c[1:-1] * around(y, 4) + around(c * y, 4))
    x2 = invd[1:-1] * (alpha * f[1:-1] + s)
    coarse = x2[1:5, 4:8]
    total = c[2:-2] * around(x2, 4) + around(c[1:-1] * x2, 4)
    r2 = (1.0 - alpha) * f[2:-2] - s[1:-1] + 0.125 * total

    pool2[0], pool2[1] = r2[0] + r2[1], r2[2] + r2[3]
    both = pool2[:, pl.ds(4, 2, stride=2), :] + pool2[:, pl.ds(5, 2, stride=2), :]
    upper = both[0] + turn(both[0], -4)
    lower = turn(both[1], 1) + turn(both[1], -3)
    f3[...] = 0.125 * jnp.where(lanes_of(upper) % 2 == 0, upper, lower)

    def share(k, owner):
        return pltpu.make_async_remote_copy(
            src_ref=f3, dst_ref=gather_ref.at[owner], send_sem=send_d.at[k], recv_sem=recv_d.at[k],
            device_id=mate(k), device_id_type=MESH,
        )

    for k in mates:
        share(k, g).start()

    gather_ref[g] = f3[...]
    flat = middle.reshape(H1 * W1, LANES)
    for side in range(2):
        rows = squeeze(flat, 2, side).reshape(H1, W1, LANES // 2)
        for i in range(H1):
            middle_ref[2 * i + side] = rows[i]
    for i in range(4):
        coarse_ref[i] = squeeze(coarse[i], 4)

    each(stage_c, lambda copy: copy.wait_send())
    for k in mates:
        share(k, g).wait_send()
    for k in reversed(mates):
        share(k, lax.rem(g + groups - k, groups)).wait_recv()


def finish_kernel(fine, middle, coarse, gathered, fine_out, middle_out, coarse_out, rhs_out, rhs, sem):
    copies = [
        pltpu.make_async_copy(source, target, sem.at[i])
        for i, (source, target) in enumerate(((fine, fine_out), (middle, middle_out), (coarse, coarse_out)))
    ]
    for copy in copies:
        copy.start()
    depth = rhs.shape[1]
    row = lax.broadcasted_iota(jnp.int32, (2 * depth, LANES), 0)
    lane = lax.broadcasted_iota(jnp.int32, (2 * depth, LANES), 1)
    pick = lane == 8 * (row % depth) + row // depth
    both = lax.dot_general(
        pick.astype(jnp.float32), gathered[...].reshape(-1, LANES), (((1,), (1,)), ((), ())),
        precision=lax.Precision.HIGHEST, preferred_element_type=jnp.float32,
    )
    rhs[0], rhs[1] = both[:depth], both[depth:]
    last = pltpu.make_async_copy(rhs, rhs_out, sem.at[3])
    last.start()
    for copy in (*copies, last):
        copy.wait()


def solution(mesh):
    bricks, groups = mesh.shape["brick"], mesh.shape["group"]
    anywhere = pl.BlockSpec(memory_space=pl.ANY)
    vmem = pl.BlockSpec(memory_space=pltpu.VMEM)

    def buf(*shape):
        return pltpu.VMEM(shape, jnp.float32)

    dma = pltpu.SemaphoreType.DMA

    def body(right_side, mass_coef, face_coef):
        small = ((W0, W0, LANES), (W1, W1, LANES // 2), (4, 4, LANES // 4))
        held = pl.pallas_call(
            functools.partial(main_kernel, bricks, groups),
            out_shape=(*(buf(*shape) for shape in small), buf(groups, 2, LANES)),
            in_specs=[anywhere] * 3,
            out_specs=(vmem,) * 4,
            scratch_shapes=[
                buf(3, *E0), buf(2, *E1), buf(*E1),
                *([buf(*E0)] * 6), buf(E0[0], W0, LANES),
                buf(2, 4, W0, LANES), buf(12, 24, LANES), buf(2, 12, LANES), buf(2, LANES),
                dma((3,)), dma((8, 2)), dma((8, 2)), dma((8,)), dma((8,)), dma((8,)), dma((8,)),
                dma((groups,)), dma((groups,)),
            ],
            compiler_params=pltpu.CompilerParams(collective_id=0, has_side_effects=True),
            name="cycle",
        )(right_side, mass_coef, face_coef)
        held = [pltpu.with_memory_space_constraint(array, pltpu.VMEM) for array in held]
        rhs_shape = (2, LANES // 8, 2 * groups)
        fine, middle, coarse, rhs = pl.pallas_call(
            finish_kernel,
            out_shape=tuple(jax.ShapeDtypeStruct(shape, jnp.float32) for shape in (*small, rhs_shape)),
            in_specs=[vmem] * 4,
            out_specs=(anywhere,) * 4,
            scratch_shapes=[buf(*rhs_shape), dma((4,))],
            name="finish",
        )(*held)
        return fine, middle, coarse, jnp.swapaxes(rhs, 1, 2)

    placed = P("brick", "group", None)
    return jax.shard_map(
        body,
        mesh=mesh,
        in_specs=(placed, placed, placed),
        out_specs=(placed, placed, placed, P("brick", None, None)),
        check_vma=False,
    )
```

time: 34.1 us -> 26.2 us (0.77)
  local copies, waits for them, and re-layouts: 5.16 us -> 0 us
  Pallas kernels: 28.1 us -> 25.4 us
    unnamed x14 -> x0, local copies, waits for them, and re-layouts: 5.16 us -> none
    pallas_call x1, Pallas kernels: 26.4 us -> 24.6 us  [body(): pl.pallas_call(functools.partial(main_kernel, bricks, groups), out_shape=...]
    pallas_call x1, Pallas kernels: 1.7 us -> 0.8 us  [body(): pl.pallas_call(finish_kernel, out_shape=tuple((jax.ShapeDtypeStruct(shape...]
where the time goes in v2:
time: 26.2 us; the launch traced here: 26 us
  Pallas kernels  25.4 us (97%)
  between operations  0.64 us (2%)
    pallas_call x1, Pallas kernels, body(): pl.pallas_call(functools.partial(main_kernel, bricks, groups), out_shape=...  24.6 us
    pallas_call x1, Pallas kernels, body(): pl.pallas_call(finish_kernel, out_shape=tuple((jax.ShapeDtypeStruct(shape...  0.8 us

profile of v2, /device:TPU:199, one launch (start us, length us, event | category | flops | bytes accessed | tf_op | source)
XLA Modules:
  0.0 26.0 jit_solution(38365267077583521)
XLA Ops:
  0.6 24.6 %cycle.1 = (f32[16,16,128]{2,1,0:T(8,128)S(1)}, f32[8,8,64]{2,1,0:T(8,128)S(1)}, f32[4,4,32]{2,1,0:T(4,128)S(1)}, f32[16,2,128]{2,1,0:T(2,128)S(1)}) custom-call(f32[16,16,128]{2,1,0:T(8,128)} %f_ref.1, f32[16,16,128]{2,1,0:T(8,128)} %m_ref.1, f32[16,16,128]{2,1,0:T(8,128)} %c_ref.1), custom_call_target="tpu_custom_call" | custom-call | tf_op jit(solution)/shard_map/cycle/pallas_call | solution.py:353
  25.2 0.8 %finish.1 = (f32[16,16,128]{2,1,0:T(8,128)}, f32[8,8,64]{2,1,0:T(8,128)}, f32[4,4,32]{2,1,0:T(4,128)}, f32[2,16,32]{2,1,0:T(8,128)}) custom-call(f32[16,16,128]{2,1,0:T(8,128)S(1)} %get-tuple-element.12.fine, f32[8,8,64]{2,1,0:T(8,128)S(1)} %get-tuple-element.13.middle, f32[4,4,32]{2,1,0:T(4,128)S(1)} %get-tuple-element.14.coarse, ...), custom_call_target="tpu_custom_call" | custom-call | tf_op jit(solution)/shard_map/finish/pallas_call | solution.py:370

commit v3 on v2

--- a/solution.py
+++ b/solution.py
@@ -101,8 +101,8 @@
     bricks, groups,
     f_ref, m_ref, c_ref,
     fine_ref, middle_ref, coarse_ref, gather_ref,
-    x0, x1, f1, inv0, y0, cy0, x20, cx20, base0, r0, pool0, pool1, pool2, f3,
-    load_sem, send_a, recv_a, send_b, recv_b, send_c, recv_c, send_d, recv_d,
+    x0, x1, f1, inv0, y0, cy0, x20, cx20, base0, r0, pool0, pool1, pool2, f3, tally,
+    load_sem, send_sem, side_sem, recv_sem,
 ):
     b, g = lax.axis_index("brick"), lax.axis_index("group")
     barrier = pltpu.get_barrier_semaphore()
@@ -130,11 +130,25 @@
         pl.semaphore_signal(barrier, inc=1, device_id=mate(k), device_id_type=MESH)
 
     loads = [
-        pltpu.make_async_copy(ref, x0.at[i, pl.ds(I0, W0), pl.ds(J0, W0), :], load_sem.at[i])
+        pltpu.make_async_copy(ref, x0.at[i, pl.ds(I0, W0), pl.ds(J0, W0), :], load_sem)
         for i, ref in enumerate((f_ref, m_ref, c_ref))
     ]
     for copy in loads:
         copy.start()
+
+    def drain(sem, rows):
+        part = tally.at[pl.ds(0, rows)]
+        pltpu.make_async_copy(part, part, sem).wait()
+
+    def drain_by_place(sem, rows_of, keep=True):
+        wide, deep = (b > 0) & (b < bricks - 1), (g > 0) & (g < groups - 1)
+        for nb in (1, 2):
+            for ng in (1, 2):
+                here = (wide if nb == 2 else ~wide) & (deep if ng == 2 else ~deep)
+
+                @pl.when(here & keep)
+                def _():
+                    drain(sem, rows_of(nb, ng))
 
     def blank(rows0, cols0, rows1, cols1):
         shape0, shape1 = (rows0.size, cols0.size, LANES), (rows1.size, cols1.size, LANES)
@@ -162,9 +176,8 @@
     def _():
         blank(every[0], pl.ds(J0 + W0, J0), every[2], pl.ds(J1 + W1, J1))
 
-    for copy in loads:
-        copy.wait()
     own0 = (pl.ds(I0, W0), pl.ds(J0, W0))
+    drain(load_sem, 3 * W0 * W0)
     own1 = (pl.ds(I1, H1), pl.ds(J1, W1))
     x1[(0, *own1)] = pack_pool(x0[(1, *own0)], pool0)
     x1[(1, *own1)] = pack_pool(x0[(2, *own0)], pool0)
@@ -180,47 +193,37 @@
             send_sem=send, recv_sem=recv, device_id=peer, device_id_type=MESH,
         )
 
-    def stage_a(i, step, peer):
-        at, sizes = (I0, J0), (W0, W0)
-        if step[0] and step[1]:
-            return [message(x0, (pl.ds(0, 3),), step, (2, 2), at, sizes, send_a.at[i, 0], recv_a.at[i, 0], peer)]
-        return [
-            message(x0, (pl.ds(0, 2),), step, (2, 2), at, sizes, send_a.at[i, 0], recv_a.at[i, 0], peer),
-            message(x0, (2,), step, (3, 3), at, sizes, send_a.at[i, 1], recv_a.at[i, 1], peer),
-        ]
-
-    def stage_b(i, step, peer):
+    def side_of(step):
+        return side_sem.at[step[0] % 3]
+
+    def stage_a(step, peer):
+        widths = (2, 2) if step[0] and step[1] else (3, 3)
+        return message(x0, (pl.ds(0, 3),), step, widths, (I0, J0), (W0, W0), send_sem.at[0], side_of(step), peer)
+
+    def stage_b(step, peer):
         rows = 3 if step[1] else 4
-        return [message(x1, (pl.ds(0, 2),), step, (rows, W1), (I1, J1), (H1, W1), send_b.at[i], recv_b.at[i], peer)]
-
-    def stage_c(i, step, peer):
-        return [message(f1, (), step, (3, W1), (I1, J1), (H1, W1), send_c.at[i], recv_c.at[i], peer)]
-
-    def each(stage, act, keep=lambda step: True):
-        for i, step in enumerate(DIRS):
-            if keep(step):
-                ok, peer = reach(step)
-
-                @pl.when(ok)
-                def _():
-                    for copy in stage(i, step, peer):
-                        act(copy)
-
-    def receive(stage, keep=lambda step: True):
-        for i, step in reversed(list(enumerate(DIRS))):
-            if keep(step):
-                ok, peer = reach((-step[0], -step[1]))
-
-                @pl.when(ok)
-                def _():
-                    for copy in stage(i, step, peer):
-                        copy.wait_recv()
-
-    def start(copy):
-        copy.start()
-
-    each(stage_a, start)
-    each(stage_b, start)
+        return message(
+            x1, (pl.ds(0, 2),), step, (rows, W1), (I1, J1), (H1, W1), send_sem.at[1], recv_sem.at[0], peer
+        )
+
+    def stage_c(step, peer):
+        return message(f1, (), step, (3, W1), (I1, J1), (H1, W1), send_sem.at[2], recv_sem.at[1], peer)
+
+    size_a, size_b, size_c = (9 * W0, 9 * W0, 12), (8 * W1, 8 * W1, 6 * W1), (3 * W1, 4 * W1, 3 * W1)
+
+    def all_of(size):
+        return lambda nb, ng: nb * size[0] + ng * size[1] + nb * ng * size[2]
+
+    def each(stage):
+        for step in DIRS:
+            ok, peer = reach(step)
+
+            @pl.when(ok)
+            def _():
+                stage(step, peer).start()
+
+    each(stage_a)
+    each(stage_b)
 
     def diagonal(a, z):
         f, m, c = x0[0, a:z], x0[1, a:z], x0[2, a - 1 : z + 1]
@@ -239,32 +242,32 @@
         total = c * around(x20[a - 1 : z + 1], 1) + around(cx20[a - 1 : z + 1], 1)
         r0[a:z] = (base0[a:z] + 0.125 * total)[:, J0 : J0 + W0]
 
-    receive(stage_a, lambda step: step[0] == 0)
+    drain_by_place(side_sem.at[0], lambda nb, ng: ng * size_a[1])
     diagonal(4, 18)
     second(5, 17)
     residual(6, 16)
-    receive(stage_a, lambda step: step[0] == 1)
+    drain_by_place(side_sem.at[1], lambda nb, ng: size_a[0] + ng * size_a[2], b > 0)
     diagonal(1, 4)
     second(2, 5)
     residual(3, 6)
-    receive(stage_a, lambda step: step[0] == -1)
+    drain_by_place(side_sem.at[2], lambda nb, ng: size_a[0] + ng * size_a[2], b < bricks - 1)
     diagonal(18, 21)
     second(17, 20)
     residual(16, 19)
     f1[own1] = pack_pool(r0[I0 : I0 + W0], pool0)
-    each(stage_c, start)
+    each(stage_c)
     fine_ref[...] = x20[(pl.ds(I0, W0), pl.ds(J0, W0))]
 
-    receive(stage_b)
+    drain_by_place(recv_sem.at[0], all_of(size_b))
     m1, c1 = x1[0], x1[1]
     c2 = unpack_pool(c1, pool1)
     m2 = unpack_pool(m1, pool1)
     invd1 = inverse(m1[1:-1], c1[1:-1], around_pairs(c1, 2))
     invd2 = inverse(m2[1:-1], c2[1:-1], around(c2, 4))
-    each(stage_a, lambda copy: copy.wait_send())
-    each(stage_b, lambda copy: copy.wait_send())
-
-    receive(stage_c)
+    drain_by_place(send_sem.at[0], all_of(size_a))
+    drain_by_place(send_sem.at[1], all_of(size_b))
+
+    drain_by_place(recv_sem.at[1], all_of(size_c))
     f = f1[1:-1]
     y = f * invd1
     edge = jnp.zeros((1, *E1[1:]), jnp.float32)
@@ -291,14 +294,11 @@
     lower = turn(both[1], 1) + turn(both[1], -3)
     f3[...] = 0.125 * jnp.where(lanes_of(upper) % 2 == 0, upper, lower)
 
-    def share(k, owner):
-        return pltpu.make_async_remote_copy(
-            src_ref=f3, dst_ref=gather_ref.at[owner], send_sem=send_d.at[k], recv_sem=recv_d.at[k],
+    for k in mates:
+        pltpu.make_async_remote_copy(
+            src_ref=f3, dst_ref=gather_ref.at[g], send_sem=send_sem.at[3], recv_sem=recv_sem.at[2],
             device_id=mate(k), device_id_type=MESH,
-        )
-
-    for k in mates:
-        share(k, g).start()
+        ).start()
 
     gather_ref[g] = f3[...]
     flat = middle.reshape(H1 * W1, LANES)
@@ -309,11 +309,9 @@
     for i in range(4):
         coarse_ref[i] = squeeze(coarse[i], 4)
 
-    each(stage_c, lambda copy: copy.wait_send())
-    for k in mates:
-        share(k, g).wait_send()
-    for k in reversed(mates):
-        share(k, lax.rem(g + groups - k, groups)).wait_recv()
+    drain_by_place(send_sem.at[2], all_of(size_c))
+    drain(send_sem.at[3], 2 * (groups - 1))
+    drain(recv_sem.at[2], 2 * (groups - 1))
 
 
 def finish_kernel(fine, middle, coarse, gathered, fine_out, middle_out, coarse_out, rhs_out, rhs, sem):
@@ -359,8 +357,7 @@
                 buf(3, *E0), buf(2, *E1), buf(*E1),
                 *([buf(*E0)] * 6), buf(E0[0], W0, LANES),
                 buf(2, 4, W0, LANES), buf(12, 24, LANES), buf(2, 12, LANES), buf(2, LANES),
-                dma((3,)), dma((8, 2)), dma((8, 2)), dma((8,)), dma((8,)), dma((8,)), dma((8,)),
-                dma((groups,)), dma((groups,)),
+                buf(3 * W0 * W0, LANES), dma, dma((4,)), dma((3,)), dma((3,)),
             ],
             compiler_params=pltpu.CompilerParams(collective_id=0, has_side_effects=True),
             name="cycle",

time: 26.2 us -> 25.6 us (0.977)
  Pallas kernels: 25.4 us -> 24.9 us
    pallas_call x1, Pallas kernels: 24.6 us -> 24.1 us  [body(): pl.pallas_call(functools.partial(main_kernel, bricks, groups), out_shape=...]
where the time goes in v3:
time: 25.6 us; the launch traced here: 25.5 us
  Pallas kernels  24.9 us (97%)
  between operations  0.64 us (2%)
    pallas_call x1, Pallas kernels, body(): pl.pallas_call(functools.partial(main_kernel, bricks, groups), out_shape=...  24.1 us
    pallas_call x1, Pallas kernels, body(): pl.pallas_call(finish_kernel, out_shape=tuple((jax.ShapeDtypeStruct(shape...  0.8 us

profile of v3, /device:TPU:199, one launch (start us, length us, event | category | flops | bytes accessed | tf_op | source)
XLA Modules:
  0.0 25.5 jit_solution(6410366020675941065)
XLA Ops:
  0.6 24.1 %cycle.1 = (f32[16,16,128]{2,1,0:T(8,128)S(1)}, f32[8,8,64]{2,1,0:T(8,128)S(1)}, f32[4,4,32]{2,1,0:T(4,128)S(1)}, f32[16,2,128]{2,1,0:T(2,128)S(1)}) custom-call(f32[16,16,128]{2,1,0:T(8,128)} %f_ref.1, f32[16,16,128]{2,1,0:T(8,128)} %m_ref.1, f32[16,16,128]{2,1,0:T(8,128)} %c_ref.1), custom_call_target="tpu_custom_call" | custom-call | tf_op jit(solution)/shard_map/cycle/pallas_call | solution.py:351
  24.7 0.8 %finish.1 = (f32[16,16,128]{2,1,0:T(8,128)}, f32[8,8,64]{2,1,0:T(8,128)}, f32[4,4,32]{2,1,0:T(4,128)}, f32[2,16,32]{2,1,0:T(8,128)}) custom-call(f32[16,16,128]{2,1,0:T(8,128)S(1)} %get-tuple-element.12.fine, f32[8,8,64]{2,1,0:T(8,128)S(1)} %get-tuple-element.13.middle, f32[4,4,32]{2,1,0:T(4,128)S(1)} %get-tuple-element.14.coarse, ...), custom_call_target="tpu_custom_call" | custom-call | tf_op jit(solution)/shard_map/finish/pallas_call | solution.py:367

commit v4 on v3

--- a/solution.py
+++ b/solution.py
@@ -22,10 +22,11 @@
 
 OUTSIDE_MASS = 1e30
 LANES = 128
-I0, J0, W0, E0 = 3, 8, 16, (22, 32, LANES)
+I0, J0, W0, E0 = 3, 12, 16, (22, 40, LANES)
+J8 = pl.ds(8, 24)
 I1, H1, J1, W1, E1 = 4, 4, 8, 8, (12, 24, LANES)
 
-DIRS = [(1, 0), (-1, 0), (1, 1), (1, -1), (-1, 1), (-1, -1), (0, 1), (0, -1)]
+DIRS = [(1, 1), (1, -1), (-1, 1), (-1, -1), (1, 0), (-1, 0), (0, 1), (0, -1)]
 
 
 def cut(step, start, size, width):
@@ -52,14 +53,53 @@
     return low + high + pltpu.roll(mid, 1, axis=1) + pltpu.roll(mid, cols - 1, axis=1)
 
 
+def around_at(ref, at, n):
+    mid = ref[pl.ds(at, n), J8]
+    lane = lanes_of(mid)
+    low, high = jnp.where(lane >= 1, turn(mid, 1), 0.0), jnp.where(lane < LANES - 1, turn(mid, -1), 0.0)
+    rows = ref[pl.ds(at - 1, n), J8] + ref[pl.ds(at + 1, n), J8]
+    return rows + (ref[pl.ds(at, n), pl.ds(7, 24)] + ref[pl.ds(at, n), pl.ds(9, 24)]) + (low + high)
+
+
 def around(a, by):
     return a[2:] + a[:-2] + beside(a[1:-1], by)
 
 
-def around_pairs(a, by):
+def rows_beside(a):
+    return a[:-2], a[2:]
+
+
+def pairs_beside(a):
     up, down = turn(a[:-1], -1), turn(a[1:], 1)
     even = lanes_of(a[1:-1]) % 2 == 0
-    return jnp.where(even, up[1:] + up[:-1], down[1:] + down[:-1]) + beside(a[1:-1], by)
+    return jnp.where(even, up[:-1], down[:-1]), jnp.where(even, up[1:], down[1:])
+
+
+def six(a, by, rows):
+    mid = a[1:-1]
+    return (
+        *rows(a), pltpu.roll(mid, 1, axis=1), pltpu.roll(mid, mid.shape[1] - 1, axis=1), turn(mid, by), turn(mid, -by)
+    )
+
+
+def weigh(c, by, rows, out):
+    mid = c[1:-1]
+    lane = lanes_of(mid)
+    total = None
+    for i, near in enumerate(six(c, by, rows)):
+        inside = {4: lane >= by, 5: lane < LANES - by}.get(i)
+        if inside is not None:
+            near = jnp.where(inside, near, 0.0)
+        weight = 0.125 * (mid + near)
+        out[i] = weight if inside is None else jnp.where(inside, weight, 0.0)
+        total = near if total is None else total + near
+    return total
+
+
+def spread(u, by, rows, weights):
+    near = six(u, by, rows)
+    parts = [weights(i) * near[i] for i in range(6)]
+    return ((parts[0] + parts[1]) + (parts[2] + parts[3])) + (parts[4] + parts[5])
 
 
 def inverse(m, c, total):
@@ -77,16 +117,19 @@
     )
 
 
-def halve(a, scratch):
+def halve(a, scratch, first=0, count=None):
     rows, cols, _ = a.shape
+    count = count or cols // 2
     scratch[0:rows, 0:cols, :] = a
-    return scratch[0:rows, pl.ds(0, cols // 2, stride=2), :] + scratch[0:rows, pl.ds(1, cols // 2, stride=2), :]
-
-
-def pack_pool(a, scratch):
+    even, odd = pl.ds(first, count, stride=2), pl.ds(first + 1, count, stride=2)
+    return scratch[0:rows, even, :] + scratch[0:rows, odd, :]
+
+
+def pack_pool(a, scratch, first=0):
     rows, cols, _ = a.shape
     quad = a.reshape(rows // 4, 4, cols, LANES)
-    upper, lower = halve(quad[:, 0] + quad[:, 1], scratch.at[0]), halve(quad[:, 2] + quad[:, 3], scratch.at[1])
+    upper = halve(quad[:, 0] + quad[:, 1], scratch.at[0], first, W1)
+    lower = halve(quad[:, 2] + quad[:, 3], scratch.at[1], first, W1)
     even = lanes_of(upper) % 2 == 0
     return 0.125 * jnp.where(even, upper + turn(upper, -1), lower + turn(lower, 1))
 
@@ -101,8 +144,8 @@
     bricks, groups,
     f_ref, m_ref, c_ref,
     fine_ref, middle_ref, coarse_ref, gather_ref,
-    x0, x1, f1, inv0, y0, cy0, x20, cx20, base0, r0, pool0, pool1, pool2, f3, tally,
-    load_sem, send_sem, side_sem, recv_sem,
+    x0, x1, f1, inv0, y0, cy0, x20, cx20, base0, r0, pool0, pool1, pool2, f3, tally, w1, w2, invd1, invd2,
+    load_sem, send_sem, side_sem, recv_sem, word_sem,
 ):
     b, g = lax.axis_index("brick"), lax.axis_index("group")
     barrier = pltpu.get_barrier_semaphore()
@@ -117,7 +160,7 @@
 
     mates = sorted(range(1, groups), key=lambda k: (abs(2 * k - groups), k))
 
-    expected = groups - 1
+    expected = 2
     for step in DIRS[:6]:
         ok, peer = reach(step)
         expected = expected + ok.astype(jnp.int32)
@@ -126,8 +169,21 @@
         def _():
             pl.semaphore_signal(barrier, inc=1, device_id=peer, device_id_type=MESH)
 
-    for k in mates:
+    for k in (1, groups - 1):
         pl.semaphore_signal(barrier, inc=1, device_id=mate(k), device_id_type=MESH)
+
+    hops = []
+    while 2 ** len(hops) < groups // 2:
+        hops.append(2 ** len(hops))
+
+    def tell(i):
+        if i < len(hops):
+            for k in (hops[i], groups - hops[i]):
+                pl.semaphore_signal(word_sem.at[i], inc=1, device_id=mate(k), device_id_type=MESH)
+
+    def hear(i):
+        if i < len(hops):
+            pl.semaphore_wait(word_sem.at[i], 2)
 
     loads = [
         pltpu.make_async_copy(ref, x0.at[i, pl.ds(I0, W0), pl.ds(J0, W0), :], load_sem)
@@ -197,19 +253,23 @@
         return side_sem.at[step[0] % 3]
 
     def stage_a(step, peer):
-        widths = (2, 2) if step[0] and step[1] else (3, 3)
-        return message(x0, (pl.ds(0, 3),), step, widths, (I0, J0), (W0, W0), send_sem.at[0], side_of(step), peer)
+        def part(lead, width):
+            return message(
+                x0, (lead,), step, (width, width), (I0, J0), (W0, W0), send_sem.at[0], side_of(step), peer
+            )
+
+        return [part(pl.ds(0, 3), 2)] if step[0] and step[1] else [part(pl.ds(0, 2), 2), part(2, 3)]
 
     def stage_b(step, peer):
         rows = 3 if step[1] else 4
-        return message(
+        return [message(
             x1, (pl.ds(0, 2),), step, (rows, W1), (I1, J1), (H1, W1), send_sem.at[1], recv_sem.at[0], peer
-        )
+        )]
 
     def stage_c(step, peer):
-        return message(f1, (), step, (3, W1), (I1, J1), (H1, W1), send_sem.at[2], recv_sem.at[1], peer)
-
-    size_a, size_b, size_c = (9 * W0, 9 * W0, 12), (8 * W1, 8 * W1, 6 * W1), (3 * W1, 4 * W1, 3 * W1)
+        return [message(f1, (), step, (3, W1), (I1, J1), (H1, W1), send_sem.at[2], recv_sem.at[1], peer)]
+
+    size_a, size_b, size_c = (7 * W0, 7 * W0, 12), (8 * W1, 8 * W1, 6 * W1), (3 * W1, 4 * W1, 3 * W1)
 
     def all_of(size):
         return lambda nb, ng: nb * size[0] + ng * size[1] + nb * ng * size[2]
@@ -220,73 +280,83 @@
 
             @pl.when(ok)
             def _():
-                stage(step, peer).start()
-
+                for copy in stage(step, peer):
+                    copy.start()
+
+    tell(0)
     each(stage_a)
     each(stage_b)
-
-    def diagonal(a, z):
-        f, m, c = x0[0, a:z], x0[1, a:z], x0[2, a - 1 : z + 1]
-        invd = inverse(m, c[1:-1], around(c, 1))
+    hear(0)
+    tell(1)
+
+    def diagonal(at, n):
+        rows = pl.ds(at, n)
+        f, m, c = x0[0, rows, J8], x0[1, rows, J8], x0[2, rows, J8]
+        invd = inverse(m, c, around_at(x0.at[2], at, n))
         y = f * invd
-        inv0[a:z], y0[a:z], cy0[a:z] = invd, y, c[1:-1] * y
-
-    def second(a, z):
-        f, c = x0[0, a:z], x0[2, a:z]
-        s = (0.125 * beta) * (c * around(y0[a - 1 : z + 1], 1) + around(cy0[a - 1 : z + 1], 1))
-        x2 = inv0[a:z] * (alpha * f + s)
-        x20[a:z], cx20[a:z], base0[a:z] = x2, c * x2, (1.0 - alpha) * f - s
-
-    def residual(a, z):
-        c = x0[2, a:z]
-        total = c * around(x20[a - 1 : z + 1], 1) + around(cx20[a - 1 : z + 1], 1)
-        r0[a:z] = (base0[a:z] + 0.125 * total)[:, J0 : J0 + W0]
+        inv0[rows, J8], y0[rows, J8], cy0[rows, J8] = invd, y, c * y
+
+    def second(at, n):
+        rows = pl.ds(at, n)
+        f, c = x0[0, rows, J8], x0[2, rows, J8]
+        s = (0.125 * beta) * (c * around_at(y0, at, n) + around_at(cy0, at, n))
+        x2 = inv0[rows, J8] * (alpha * f + s)
+        x20[rows, J8], cx20[rows, J8], base0[rows, J8] = x2, c * x2, (1.0 - alpha) * f - s
+
+    def residual(at, n):
+        rows = pl.ds(at, n)
+        total = x0[2, rows, J8] * around_at(x20, at, n) + around_at(cx20, at, n)
+        r0[rows] = base0[rows, J8] + 0.125 * total
 
     drain_by_place(side_sem.at[0], lambda nb, ng: ng * size_a[1])
-    diagonal(4, 18)
-    second(5, 17)
-    residual(6, 16)
-    drain_by_place(side_sem.at[1], lambda nb, ng: size_a[0] + ng * size_a[2], b > 0)
-    diagonal(1, 4)
-    second(2, 5)
-    residual(3, 6)
-    drain_by_place(side_sem.at[2], lambda nb, ng: size_a[0] + ng * size_a[2], b < bricks - 1)
-    diagonal(18, 21)
-    second(17, 20)
-    residual(16, 19)
-    f1[own1] = pack_pool(r0[I0 : I0 + W0], pool0)
+    diagonal(4, 14)
+    second(5, 12)
+    residual(6, 10)
+    f1[pl.ds(I1 + 1, 2), pl.ds(J1, W1), :] = pack_pool(r0[7:15], pool0, J0 - 8)
+    hear(1)
+    tell(2)
+    run = 4
+    for turn_no in range(2):
+        low = (lax.rem(b, run) != 0) if turn_no == 0 else (lax.rem(b, run) == 0)
+
+        def arrived(nb, ng):
+            return size_a[0] + ng * size_a[2]
+
+        drain_by_place(side_sem.at[1], arrived, low & (b > 0))
+        drain_by_place(side_sem.at[2], arrived, ~low & (b < bricks - 1))
+        diagonal(jnp.where(low, 1, 18), 3)
+        second(jnp.where(low, 2, 17), 3)
+        residual(jnp.where(low, 3, 16), 3)
+        quad = pack_pool(r0[pl.ds(jnp.where(low, 3, 15), 4)], pool0, J0 - 8)
+        f1[pl.ds(jnp.where(low, I1, I1 + 3), 1), pl.ds(J1, W1), :] = quad
     each(stage_c)
-    fine_ref[...] = x20[(pl.ds(I0, W0), pl.ds(J0, W0))]
+    fine_ref[...] = x20[own0]
 
     drain_by_place(recv_sem.at[0], all_of(size_b))
     m1, c1 = x1[0], x1[1]
     c2 = unpack_pool(c1, pool1)
     m2 = unpack_pool(m1, pool1)
-    invd1 = inverse(m1[1:-1], c1[1:-1], around_pairs(c1, 2))
-    invd2 = inverse(m2[1:-1], c2[1:-1], around(c2, 4))
+    invd1[...] = inverse(m1[1:-1], c1[1:-1], weigh(c1, 2, pairs_beside, w1))
+    invd2[...] = inverse(m2[1:-1], c2[1:-1], weigh(c2, 4, rows_beside, w2))
     drain_by_place(send_sem.at[0], all_of(size_a))
     drain_by_place(send_sem.at[1], all_of(size_b))
 
     drain_by_place(recv_sem.at[1], all_of(size_c))
     f = f1[1:-1]
-    y = f * invd1
+    invd = invd1[...]
     edge = jnp.zeros((1, *E1[1:]), jnp.float32)
-    y = jnp.concatenate([edge, y, edge], axis=0)
-    s = (0.125 * beta) * (c1[1:-1] * around_pairs(y, 2) + around_pairs(c1 * y, 2))
-    x2 = invd1 * (alpha * f + s)
+    y = jnp.concatenate([edge, f * invd, edge], axis=0)
+    s = beta * spread(y, 2, pairs_beside, lambda i: w1[i])
+    x2 = invd * (alpha * f + s)
     middle = x2[3:7, J1 : J1 + W1]
-    cx2 = c1[1:-1] * x2
-    total = c1[2:-2] * around_pairs(x2, 2) + around_pairs(cx2, 2)
-    r2 = (1.0 - alpha) * f[1:-1] - s[1:-1] + 0.125 * total
+    r2 = (1.0 - alpha) * f[1:-1] - s[1:-1] + spread(x2, 2, pairs_beside, lambda i: w1[i, 1:9])
 
     f = unpack_pool(r2, pool1)
-    c, invd = c2[2:10], invd2[1:9]
-    y = f * invd
-    s = (0.125 * beta) * (c[1:-1] * around(y, 4) + around(c * y, 4))
+    invd = invd2[1:9]
+    s = beta * spread(f * invd, 4, rows_beside, lambda i: w2[i, 2:8])
     x2 = invd[1:-1] * (alpha * f[1:-1] + s)
     coarse = x2[1:5, 4:8]
-    total = c[2:-2] * around(x2, 4) + around(c[1:-1] * x2, 4)
-    r2 = (1.0 - alpha) * f[2:-2] - s[1:-1] + 0.125 * total
+    r2 = (1.0 - alpha) * f[2:-2] - s[1:-1] + spread(x2, 4, rows_beside, lambda i: w2[i, 3:7])
 
     pool2[0], pool2[1] = r2[0] + r2[1], r2[2] + r2[3]
     both = pool2[:, pl.ds(4, 2, stride=2), :] + pool2[:, pl.ds(5, 2, stride=2), :]
@@ -294,6 +364,7 @@
     lower = turn(both[1], 1) + turn(both[1], -3)
     f3[...] = 0.125 * jnp.where(lanes_of(upper) % 2 == 0, upper, lower)
 
+    hear(2)
     for k in mates:
         pltpu.make_async_remote_copy(
             src_ref=f3, dst_ref=gather_ref.at[g], send_sem=send_sem.at[3], recv_sem=recv_sem.at[2],
@@ -355,9 +426,11 @@
             out_specs=(vmem,) * 4,
             scratch_shapes=[
                 buf(3, *E0), buf(2, *E1), buf(*E1),
-                *([buf(*E0)] * 6), buf(E0[0], W0, LANES),
-                buf(2, 4, W0, LANES), buf(12, 24, LANES), buf(2, 12, LANES), buf(2, LANES),
-                buf(3 * W0 * W0, LANES), dma, dma((4,)), dma((3,)), dma((3,)),
+                *([buf(*E0)] * 6), buf(E0[0], 24, LANES),
+                buf(2, 4, 24, LANES), buf(12, 24, LANES), buf(2, 12, LANES), buf(2, LANES),
+                buf(3 * W0 * W0, LANES),
+                buf(6, 10, 24, LANES), buf(6, 10, 12, LANES), buf(10, 24, LANES), buf(10, 12, LANES),
+                dma, dma((4,)), dma((3,)), dma((3,)), pltpu.SemaphoreType.REGULAR((3,)),
             ],
             compiler_params=pltpu.CompilerParams(collective_id=0, has_side_effects=True),
             name="cycle",

time: 25.6 us -> 25.1 us (0.980)
  Pallas kernels: 24.9 us -> 24.3 us
    pallas_call x1, Pallas kernels: 24.1 us -> 23.5 us  [body(): pl.pallas_call(functools.partial(main_kernel, bricks, groups), out_shape=...]
where the time goes in v4:
time: 25.1 us; the launch traced here: 25 us
  Pallas kernels  24.3 us (97%)
  between operations  0.64 us (3%)
    pallas_call x1, Pallas kernels, body(): pl.pallas_call(functools.partial(main_kernel, bricks, groups), out_shape=...  23.5 us
    pallas_call x1, Pallas kernels, body(): pl.pallas_call(finish_kernel, out_shape=tuple((jax.ShapeDtypeStruct(shape...  0.8 us

profile of v4, /device:TPU:199, one launch (start us, length us, event | category | flops | bytes accessed | tf_op | source)
XLA Modules:
  0.0 25.0 jit_solution(14429358616473505873)
XLA Ops:
  0.6 23.5 %cycle.1 = (f32[16,16,128]{2,1,0:T(8,128)S(1)}, f32[8,8,64]{2,1,0:T(8,128)S(1)}, f32[4,4,32]{2,1,0:T(4,128)S(1)}, f32[16,2,128]{2,1,0:T(2,128)S(1)}) custom-call(f32[16,16,128]{2,1,0:T(8,128)} %f_ref.1, f32[16,16,128]{2,1,0:T(8,128)} %m_ref.1, f32[16,16,128]{2,1,0:T(8,128)} %c_ref.1), custom_call_target="tpu_custom_call" | custom-call | tf_op jit(solution)/shard_map/cycle/pallas_call | solution.py:422
  24.2 0.8 %finish.1 = (f32[16,16,128]{2,1,0:T(8,128)}, f32[8,8,64]{2,1,0:T(8,128)}, f32[4,4,32]{2,1,0:T(4,128)}, f32[2,16,32]{2,1,0:T(8,128)}) custom-call(f32[16,16,128]{2,1,0:T(8,128)S(1)} %get-tuple-element.12.fine, f32[8,8,64]{2,1,0:T(8,128)S(1)} %get-tuple-element.13.middle, f32[4,4,32]{2,1,0:T(4,128)S(1)} %get-tuple-element.14.coarse, ...), custom_call_target="tpu_custom_call" | custom-call | tf_op jit(solution)/shard_map/finish/pallas_call | solution.py:440

commit v5 on v4

--- a/solution.py
+++ b/solution.py
@@ -24,17 +24,20 @@
 LANES = 128
 I0, J0, W0, E0 = 3, 12, 16, (22, 40, LANES)
 J8 = pl.ds(8, 24)
+K0, PATCH = 3, (10, 16, LANES)
+J4 = pl.ds(4, 8)
+CORNERS = [(1, 1), (1, 0), (0, 1), (0, 0)]
 I1, H1, J1, W1, E1 = 4, 4, 8, 8, (12, 24, LANES)
 
 DIRS = [(1, 1), (1, -1), (-1, 1), (-1, -1), (1, 0), (-1, 0), (0, 1), (0, -1)]
 
 
-def cut(step, start, size, width):
+def cut(step, start, size, width, skip):
     if step == 0:
         return start, start, size
     if step > 0:
-        return start + size - width, start - width, width
-    return start, start + size, width
+        return start + size - width - skip, start - width - skip, width
+    return start + skip, start + size + skip, width
 
 
 def lanes_of(a):
@@ -53,12 +56,13 @@
     return low + high + pltpu.roll(mid, 1, axis=1) + pltpu.roll(mid, cols - 1, axis=1)
 
 
-def around_at(ref, at, n):
-    mid = ref[pl.ds(at, n), J8]
+def around_at(ref, at, n, cols):
+    rows = pl.ds(at, n)
+    mid = ref[rows, cols]
     lane = lanes_of(mid)
     low, high = jnp.where(lane >= 1, turn(mid, 1), 0.0), jnp.where(lane < LANES - 1, turn(mid, -1), 0.0)
-    rows = ref[pl.ds(at - 1, n), J8] + ref[pl.ds(at + 1, n), J8]
-    return rows + (ref[pl.ds(at, n), pl.ds(7, 24)] + ref[pl.ds(at, n), pl.ds(9, 24)]) + (low + high)
+    left, right = pl.ds(cols.start - 1, cols.size), pl.ds(cols.start + 1, cols.size)
+    return ref[pl.ds(at - 1, n), cols] + ref[pl.ds(at + 1, n), cols] + (ref[rows, left] + ref[rows, right]) + (low + high)
 
 
 def around(a, by):
@@ -144,7 +148,7 @@
     bricks, groups,
     f_ref, m_ref, c_ref,
     fine_ref, middle_ref, coarse_ref, gather_ref,
-    x0, x1, f1, inv0, y0, cy0, x20, cx20, base0, r0, pool0, pool1, pool2, f3, tally, w1, w2, invd1, invd2,
+    x0, x1, f1, inv0, y0, cy0, x20, cx20, base0, r0, pool0, pool1, pool2, f3, tally, w1, w2, invd1, invd2, px, work, pool3, near,
     load_sem, send_sem, side_sem, recv_sem, word_sem,
 ):
     b, g = lax.axis_index("brick"), lax.axis_index("group")
@@ -161,7 +165,7 @@
     mates = sorted(range(1, groups), key=lambda k: (abs(2 * k - groups), k))
 
     expected = 2
-    for step in DIRS[:6]:
+    for step in ((1, 0), (-1, 0)):
         ok, peer = reach(step)
         expected = expected + ok.astype(jnp.int32)
 
@@ -172,7 +176,7 @@
     for k in (1, groups - 1):
         pl.semaphore_signal(barrier, inc=1, device_id=mate(k), device_id_type=MESH)
 
-    hops = []
+    hops = [1]
     while 2 ** len(hops) < groups // 2:
         hops.append(2 ** len(hops))
 
@@ -214,23 +218,38 @@
             x1[i, rows1, cols1, :] = jnp.full(shape1, value, jnp.float32)
         f1[rows1, cols1, :] = jnp.zeros(shape1, jnp.float32)
 
+    def blank_patch(v, rows, cols):
+        for i, value in enumerate((0.0, OUTSIDE_MASS, 0.0)):
+            px[v, i, rows, cols, :] = jnp.full((rows.size, cols.size, LANES), value, jnp.float32)
+
+    def blank_patches(dim, high):
+        for v, corner in enumerate(CORNERS):
+            if corner[dim] == high:
+                rows = pl.ds(5 * high, 5) if dim == 0 else pl.ds(0, 10)
+                cols = pl.ds(K0 + 5 * high, 5) if dim == 1 else pl.ds(0, 16)
+                blank_patch(v, rows, cols)
+
     every = (pl.ds(0, E0[0]), pl.ds(0, E0[1]), pl.ds(0, E1[0]), pl.ds(0, E1[1]))
 
     @pl.when(b == 0)
     def _():
         blank(pl.ds(0, I0), every[1], pl.ds(0, I1), every[3])
+        blank_patches(0, 0)
 
     @pl.when(b == bricks - 1)
     def _():
         blank(pl.ds(I0 + W0, I0), every[1], pl.ds(I1 + H1, I1), every[3])
+        blank_patches(0, 1)
 
     @pl.when(g == 0)
     def _():
         blank(every[0], pl.ds(0, J0), every[2], pl.ds(0, J1))
+        blank_patches(1, 0)
 
     @pl.when(g == groups - 1)
     def _():
         blank(every[0], pl.ds(J0 + W0, J0), every[2], pl.ds(J1 + W1, J1))
+        blank_patches(1, 1)
 
     own0 = (pl.ds(I0, W0), pl.ds(J0, W0))
     drain(load_sem, 3 * W0 * W0)
@@ -240,9 +259,9 @@
 
     pl.semaphore_wait(barrier, expected)
 
-    def message(ref, lead, step, widths, at, sizes, send, recv, peer):
-        si, ti, ni = cut(step[0], at[0], sizes[0], widths[0])
-        sj, tj, nj = cut(step[1], at[1], sizes[1], widths[1])
+    def message(ref, lead, step, widths, at, sizes, send, recv, peer, skip=0):
+        si, ti, ni = cut(step[0], at[0], sizes[0], widths[0], skip)
+        sj, tj, nj = cut(step[1], at[1], sizes[1], widths[1], 0)
         return pltpu.make_async_remote_copy(
             src_ref=ref.at[(*lead, pl.ds(si, ni), pl.ds(sj, nj))],
             dst_ref=ref.at[(*lead, pl.ds(ti, ni), pl.ds(tj, nj))],
@@ -258,18 +277,53 @@
                 x0, (lead,), step, (width, width), (I0, J0), (W0, W0), send_sem.at[0], side_of(step), peer
             )
 
-        return [part(pl.ds(0, 3), 2)] if step[0] and step[1] else [part(pl.ds(0, 2), 2), part(2, 3)]
+        return [] if step[0] and step[1] else [part(pl.ds(0, 2), 2), part(2, 3)]
+
+    def send_corners(across):
+        for ci, cj in CORNERS:
+            for di, dj in ((0, 1), (1, 0), (1, 1)):
+                if (di and dj) != across:
+                    continue
+                step = ((2 * ci - 1) * di, (2 * cj - 1) * dj)
+                if di and dj:
+                    parts = ((pl.ds(0, 2), (0, 4), (0, 4)), (2, (0, 5), (0, 5)))
+                elif di:
+                    parts = ((pl.ds(0, 2), (2, 2), (0, 3)), (2, (3, 2), (0, 3)))
+                else:
+                    parts = ((pl.ds(0, 2), (0, 3), (2, 2)), (2, (0, 3), (3, 2)))
+                there = CORNERS.index((ci ^ di, cj ^ dj))
+                ok, peer = reach(step)
+
+                @pl.when(ok)
+                def _():
+                    for lead, (ri, ni), (rj, nj) in parts:
+                        pi, pj = (5 - ri - ni if ci else ri), (5 - rj - nj if cj else rj)
+                        pltpu.make_async_remote_copy(
+                            src_ref=x0.at[lead, pl.ds(I0 + 11 * ci + pi, ni), pl.ds(J0 + 11 * cj + pj, nj)],
+                            dst_ref=px.at[
+                                there, lead, pl.ds(5 * (1 - ci) + pi, ni), pl.ds(K0 + 5 * (1 - cj) + pj, nj)
+                            ],
+                            send_sem=send_sem.at[4], recv_sem=recv_sem.at[3], device_id=peer, device_id_type=MESH,
+                        ).start()
 
     def stage_b(step, peer):
-        rows = 3 if step[1] else 4
-        return [message(
-            x1, (pl.ds(0, 2),), step, (rows, W1), (I1, J1), (H1, W1), send_sem.at[1], recv_sem.at[0], peer
-        )]
+        def part(lead, widths, skip=0):
+            return message(
+                x1, (lead,), step, widths, (I1, J1), (H1, W1), send_sem.at[1], recv_sem.at[0], peer, skip
+            )
+
+        if step[0] and step[1]:
+            return [part(pl.ds(0, 2), (1, 6)), part(pl.ds(0, 2), (2, 4), 1)]
+        return [part(0, (3, 0)), part(1, (4, 0))] if step[0] else [part(pl.ds(0, 2), (0, 7))]
 
     def stage_c(step, peer):
-        return [message(f1, (), step, (3, W1), (I1, J1), (H1, W1), send_sem.at[2], recv_sem.at[1], peer)]
-
-    size_a, size_b, size_c = (7 * W0, 7 * W0, 12), (8 * W1, 8 * W1, 6 * W1), (3 * W1, 4 * W1, 3 * W1)
+        def part(widths, skip=0):
+            return message(f1, (), step, widths, (I1, J1), (H1, W1), send_sem.at[2], recv_sem.at[1], peer, skip)
+
+        return [part((1, 5)), part((2, 3), 1)] if step[0] and step[1] else [part((3, 6))]
+
+    size_a, size_b, size_c = (7 * W0, 7 * W0, 0), (56, 56, 28), (24, 24, 11)
+    size_k = (2 * 18, 2 * 18, 57)
 
     def all_of(size):
         return lambda nb, ng: nb * size[0] + ng * size[1] + nb * ng * size[2]
@@ -285,33 +339,40 @@
 
     tell(0)
     each(stage_a)
-    each(stage_b)
+    send_corners(0)
     hear(0)
     tell(1)
-
-    def diagonal(at, n):
+    send_corners(1)
+    each(stage_b)
+
+    block = (x0, inv0, y0, cy0, x20, cx20, base0)
+
+    def diagonal(at, n, fields=block, cols=J8):
+        x, inv, y, cy, _, _, _ = fields
         rows = pl.ds(at, n)
-        f, m, c = x0[0, rows, J8], x0[1, rows, J8], x0[2, rows, J8]
-        invd = inverse(m, c, around_at(x0.at[2], at, n))
-        y = f * invd
-        inv0[rows, J8], y0[rows, J8], cy0[rows, J8] = invd, y, c * y
-
-    def second(at, n):
+        f, m, c = x[0, rows, cols], x[1, rows, cols], x[2, rows, cols]
+        invd = inverse(m, c, around_at(x.at[2], at, n, cols))
+        first = f * invd
+        inv[rows, cols], y[rows, cols], cy[rows, cols] = invd, first, c * first
+
+    def second(at, n, fields=block, cols=J8):
+        x, inv, y, cy, x2, cx2, base = fields
         rows = pl.ds(at, n)
-        f, c = x0[0, rows, J8], x0[2, rows, J8]
-        s = (0.125 * beta) * (c * around_at(y0, at, n) + around_at(cy0, at, n))
-        x2 = inv0[rows, J8] * (alpha * f + s)
-        x20[rows, J8], cx20[rows, J8], base0[rows, J8] = x2, c * x2, (1.0 - alpha) * f - s
-
-    def residual(at, n):
+        f, c = x[0, rows, cols], x[2, rows, cols]
+        s = (0.125 * beta) * (c * around_at(y, at, n, cols) + around_at(cy, at, n, cols))
+        fix = inv[rows, cols] * (alpha * f + s)
+        x2[rows, cols], cx2[rows, cols], base[rows, cols] = fix, c * fix, (1.0 - alpha) * f - s
+
+    def residual(at, n, fields=block, cols=J8):
+        x, _, _, _, x2, cx2, base = fields
         rows = pl.ds(at, n)
-        total = x0[2, rows, J8] * around_at(x20, at, n) + around_at(cx20, at, n)
-        r0[rows] = base0[rows, J8] + 0.125 * total
+        total = x[2, rows, cols] * around_at(x2, at, n, cols) + around_at(cx2, at, n, cols)
+        return base[rows, cols] + 0.125 * total
 
     drain_by_place(side_sem.at[0], lambda nb, ng: ng * size_a[1])
     diagonal(4, 14)
     second(5, 12)
-    residual(6, 10)
+    r0[6:16] = residual(6, 10)
     f1[pl.ds(I1 + 1, 2), pl.ds(J1, W1), :] = pack_pool(r0[7:15], pool0, J0 - 8)
     hear(1)
     tell(2)
@@ -320,17 +381,34 @@
         low = (lax.rem(b, run) != 0) if turn_no == 0 else (lax.rem(b, run) == 0)
 
         def arrived(nb, ng):
-            return size_a[0] + ng * size_a[2]
+            return size_a[0]
 
         drain_by_place(side_sem.at[1], arrived, low & (b > 0))
         drain_by_place(side_sem.at[2], arrived, ~low & (b < bricks - 1))
         diagonal(jnp.where(low, 1, 18), 3)
         second(jnp.where(low, 2, 17), 3)
-        residual(jnp.where(low, 3, 16), 3)
+        r0[pl.ds(jnp.where(low, 3, 16), 3)] = residual(jnp.where(low, 3, 16), 3)
         quad = pack_pool(r0[pl.ds(jnp.where(low, 3, 15), 4)], pool0, J0 - 8)
         f1[pl.ds(jnp.where(low, I1, I1 + 3), 1), pl.ds(J1, W1), :] = quad
     each(stage_c)
     fine_ref[...] = x20[own0]
+
+    drain_by_place(recv_sem.at[3], all_of(size_k))
+    for v, (ci, cj) in enumerate(CORNERS):
+        own_i, own_j = 5 * (1 - ci), K0 + 5 * (1 - cj)
+        for lead, deep in ((pl.ds(0, 2), 2), (pl.ds(2, 1), 3)):
+            for at_i, ni, at_j, nj in ((-deep * (1 - ci), 5 + deep, 0, 5), (0, 5, 5 if cj else -deep, deep)):
+                px[v, lead, pl.ds(own_i + at_i, ni), pl.ds(own_j + at_j, nj), :] = x0[
+                    lead, pl.ds(I0 + 11 * ci + at_i, ni), pl.ds(J0 + 11 * cj + at_j, nj), :
+                ]
+        patch = (px.at[v], *(work.at[v, i] for i in range(6)))
+        diagonal(1, 8, patch, J4)
+        second(2, 6, patch, J4)
+        r2 = residual(3, 4, patch, J4)
+        pair = halve(jnp.stack([r2[0] + r2[1], r2[2] + r2[3]]), pool3.at[v], 2, 2)
+        near[v, 0] = 0.125 * (pair[0] + turn(pair[0], 1))
+        near[v, 1] = 0.125 * (pair[1] + turn(pair[1], -1))
+        fine_ref[pl.ds(15 * ci, 1), pl.ds(15 * cj, 1), :] = work[v, 3, pl.ds(5 - ci, 1), pl.ds(K0 + 5 - cj, 1), :]
 
     drain_by_place(recv_sem.at[0], all_of(size_b))
     m1, c1 = x1[0], x1[1]
@@ -341,7 +419,14 @@
     drain_by_place(send_sem.at[0], all_of(size_a))
     drain_by_place(send_sem.at[1], all_of(size_b))
 
+    drain_by_place(send_sem.at[4], all_of(size_k))
+    drain_by_place(send_sem.at[2], all_of(size_c))
     drain_by_place(recv_sem.at[1], all_of(size_c))
+    for v, (ci, cj) in enumerate(CORNERS):
+        for lower in range(2):
+            at = (I1 - 1 + H1 * ci + lower, pl.ds(J1 - 1 + W1 * cj, 2))
+            old = f1[at]
+            f1[at] = jnp.where(lanes_of(old) % 2 == 1 - lower, near[v, lower], old)
     f = f1[1:-1]
     invd = invd1[...]
     edge = jnp.zeros((1, *E1[1:]), jnp.float32)
@@ -380,7 +465,6 @@
     for i in range(4):
         coarse_ref[i] = squeeze(coarse[i], 4)
 
-    drain_by_place(send_sem.at[2], all_of(size_c))
     drain(send_sem.at[3], 2 * (groups - 1))
     drain(recv_sem.at[2], 2 * (groups - 1))
 
@@ -430,7 +514,8 @@
                 buf(2, 4, 24, LANES), buf(12, 24, LANES), buf(2, 12, LANES), buf(2, LANES),
                 buf(3 * W0 * W0, LANES),
                 buf(6, 10, 24, LANES), buf(6, 10, 12, LANES), buf(10, 24, LANES), buf(10, 12, LANES),
-                dma, dma((4,)), dma((3,)), dma((3,)), pltpu.SemaphoreType.REGULAR((3,)),
+                buf(4, 3, *PATCH), buf(4, 6, *PATCH), buf(4, 2, 8, LANES), buf(4, 2, 2, LANES),
+                dma, dma((5,)), dma((3,)), dma((4,)), pltpu.SemaphoreType.REGULAR((3,)),
             ],
             compiler_params=pltpu.CompilerParams(collective_id=0, has_side_effects=True),
             name="cycle",

time: 25.1 us -> 24.8 us (0.988)
  Pallas kernels: 24.3 us -> 24 us
    pallas_call x1, Pallas kernels: 23.5 us -> 23.2 us  [body(): pl.pallas_call(functools.partial(main_kernel, bricks, groups), out_shape=...]
where the time goes in v5:
time: 24.8 us; the launch traced here: 24.6 us
  Pallas kernels  24 us (97%)
  between operations  0.64 us (3%)
    pallas_call x1, Pallas kernels, body(): pl.pallas_call(functools.partial(main_kernel, bricks, groups), out_shape=...  23.2 us
    pallas_call x1, Pallas kernels, body(): pl.pallas_call(finish_kernel, out_shape=tuple((jax.ShapeDtypeStruct(shape...  0.8 us

profile of v5, /device:TPU:199, one launch (start us, length us, event | category | flops | bytes accessed | tf_op | source)
XLA Modules:
  0.0 24.6 jit_solution(15240583246103858269)
XLA Ops:
  0.6 23.2 %cycle.1 = (f32[16,16,128]{2,1,0:T(8,128)S(1)}, f32[8,8,64]{2,1,0:T(8,128)S(1)}, f32[4,4,32]{2,1,0:T(4,128)S(1)}, f32[16,2,128]{2,1,0:T(2,128)S(1)}) custom-call(f32[16,16,128]{2,1,0:T(8,128)} %f_ref.1, f32[16,16,128]{2,1,0:T(8,128)} %m_ref.1, f32[16,16,128]{2,1,0:T(8,128)} %c_ref.1), custom_call_target="tpu_custom_call" | custom-call | tf_op jit(solution)/shard_map/cycle/pallas_call | solution.py:506
  23.8 0.8 %finish.1 = (f32[16,16,128]{2,1,0:T(8,128)}, f32[8,8,64]{2,1,0:T(8,128)}, f32[4,4,32]{2,1,0:T(4,128)}, f32[2,16,32]{2,1,0:T(8,128)}) custom-call(f32[16,16,128]{2,1,0:T(8,128)S(1)} %get-tuple-element.12.fine, f32[8,8,64]{2,1,0:T(8,128)S(1)} %get-tuple-element.13.middle, f32[4,4,32]{2,1,0:T(4,128)S(1)} %get-tuple-element.14.coarse, ...), custom_call_target="tpu_custom_call" | custom-call | tf_op jit(solution)/shard_map/finish/pallas_call | solution.py:525

commit v6 on v5

--- a/solution.py
+++ b/solution.py
@@ -342,8 +342,6 @@
     send_corners(0)
     hear(0)
     tell(1)
-    send_corners(1)
-    each(stage_b)
 
     block = (x0, inv0, y0, cy0, x20, cx20, base0)
 
@@ -370,6 +368,8 @@
         return base[rows, cols] + 0.125 * total
 
     drain_by_place(side_sem.at[0], lambda nb, ng: ng * size_a[1])
+    send_corners(1)
+    each(stage_b)
     diagonal(4, 14)
     second(5, 12)
     r0[6:16] = residual(6, 10)

time: 24.8 us -> 23.9 us (0.964)
  Pallas kernels: 24 us -> 23.2 us
    pallas_call x1, Pallas kernels: 23.2 us -> 22.4 us  [body(): pl.pallas_call(functools.partial(main_kernel, bricks, groups), out_shape=...]
where the time goes in v6:
time: 23.9 us; the launch traced here: 23.8 us
  Pallas kernels  23.2 us (97%)
  between operations  0.64 us (3%)
    pallas_call x1, Pallas kernels, body(): pl.pallas_call(functools.partial(main_kernel, bricks, groups), out_shape=...  22.4 us
    pallas_call x1, Pallas kernels, body(): pl.pallas_call(finish_kernel, out_shape=tuple((jax.ShapeDtypeStruct(shape...  0.8 us

profile of v6, /device:TPU:199, one launch (start us, length us, event | category | flops | bytes accessed | tf_op | source)
XLA Modules:
  0.0 23.8 jit_solution(17328357197119777508)
XLA Ops:
  0.6 22.4 %cycle.1 = (f32[16,16,128]{2,1,0:T(8,128)S(1)}, f32[8,8,64]{2,1,0:T(8,128)S(1)}, f32[4,4,32]{2,1,0:T(4,128)S(1)}, f32[16,2,128]{2,1,0:T(2,128)S(1)}) custom-call(f32[16,16,128]{2,1,0:T(8,128)} %f_ref.1, f32[16,16,128]{2,1,0:T(8,128)} %m_ref.1, f32[16,16,128]{2,1,0:T(8,128)} %c_ref.1), custom_call_target="tpu_custom_call" | custom-call | tf_op jit(solution)/shard_map/cycle/pallas_call | solution.py:506
  23.0 0.8 %finish.1 = (f32[16,16,128]{2,1,0:T(8,128)}, f32[8,8,64]{2,1,0:T(8,128)}, f32[4,4,32]{2,1,0:T(4,128)}, f32[2,16,32]{2,1,0:T(8,128)}) custom-call(f32[16,16,128]{2,1,0:T(8,128)S(1)} %get-tuple-element.12.fine, f32[8,8,64]{2,1,0:T(8,128)S(1)} %get-tuple-element.13.middle, f32[4,4,32]{2,1,0:T(4,128)S(1)} %get-tuple-element.14.coarse, ...), custom_call_target="tpu_custom_call" | custom-call | tf_op jit(solution)/shard_map/finish/pallas_call | solution.py:525

commit v7 on v6

--- a/solution.py
+++ b/solution.py
@@ -254,8 +254,6 @@
     own0 = (pl.ds(I0, W0), pl.ds(J0, W0))
     drain(load_sem, 3 * W0 * W0)
     own1 = (pl.ds(I1, H1), pl.ds(J1, W1))
-    x1[(0, *own1)] = pack_pool(x0[(1, *own0)], pool0)
-    x1[(1, *own1)] = pack_pool(x0[(2, *own0)], pool0)
 
     pl.semaphore_wait(barrier, expected)
 
@@ -340,6 +338,8 @@
     tell(0)
     each(stage_a)
     send_corners(0)
+    x1[(0, *own1)] = pack_pool(x0[(1, *own0)], pool0)
+    x1[(1, *own1)] = pack_pool(x0[(2, *own0)], pool0)
     hear(0)
     tell(1)
 

time: 23.9 us -> 23.9 us (level)
  no operation moved by 1% of the time
where the time goes in v7:
time: 23.9 us; the launch traced here: 23.8 us
  Pallas kernels  23.2 us (97%)
  between operations  0.64 us (3%)
    pallas_call x1, Pallas kernels, body(): pl.pallas_call(functools.partial(main_kernel, bricks, groups), out_shape=...  22.4 us
    pallas_call x1, Pallas kernels, body(): pl.pallas_call(finish_kernel, out_shape=tuple((jax.ShapeDtypeStruct(shape...  0.8 us

profile of v7, /device:TPU:199, one launch (start us, length us, event | category | flops | bytes accessed | tf_op | source)
XLA Modules:
  0.0 23.8 jit_solution(17107263877945064872)
XLA Ops:
  0.6 22.4 %cycle.1 = (f32[16,16,128]{2,1,0:T(8,128)S(1)}, f32[8,8,64]{2,1,0:T(8,128)S(1)}, f32[4,4,32]{2,1,0:T(4,128)S(1)}, f32[16,2,128]{2,1,0:T(2,128)S(1)}) custom-call(f32[16,16,128]{2,1,0:T(8,128)} %f_ref.1, f32[16,16,128]{2,1,0:T(8,128)} %m_ref.1, f32[16,16,128]{2,1,0:T(8,128)} %c_ref.1), custom_call_target="tpu_custom_call" | custom-call | tf_op jit(solution)/shard_map/cycle/pallas_call | solution.py:506
  23.0 0.8 %finish.1 = (f32[16,16,128]{2,1,0:T(8,128)}, f32[8,8,64]{2,1,0:T(8,128)}, f32[4,4,32]{2,1,0:T(4,128)}, f32[2,16,32]{2,1,0:T(8,128)}) custom-call(f32[16,16,128]{2,1,0:T(8,128)S(1)} %get-tuple-element.12.fine, f32[8,8,64]{2,1,0:T(8,128)S(1)} %get-tuple-element.13.middle, f32[4,4,32]{2,1,0:T(4,128)S(1)} %get-tuple-element.14.coarse, ...), custom_call_target="tpu_custom_call" | custom-call | tf_op jit(solution)/shard_map/finish/pallas_call | solution.py:525
